TPU v7x, 128 devices: a whole 4x4x4 slice. The times are simulated.
128 devices in a mesh: ctx: 32 (over x, y, z_hi), wsh: 4 (over z_lo, core).
Axes of the slice: x: 4, y: 4, z: 4 (z_hi: 2, z_lo: 2; z = z_hi * 2 + z_lo), core: 2. Of those that a mesh axis runs over, the one named last changes fastest.
Arguments:
- tokens: bfloat16 [4, 4096, 1024], P('wsh', 'ctx'), may hold values from -6 to 6
- places: int32 [4, 4096], P('wsh', 'ctx'), may hold values from 0 to 4095, as said below
- w_qkv: bfloat16 [1024, 3072], P('wsh'), may hold values from -0.1875 to 0.1875
- b_qv: bfloat16 [2048], P('wsh'), may hold values from -3 to 3
- w_out: bfloat16 [1024, 1024], P('wsh'), may hold values from -0.5 to 0.5
- b_out: bfloat16 [1024], P('wsh'), may hold values from -3 to 3
- norm1_gain: bfloat16 [1024], P('wsh'), may hold values from 0.5 to 1.5
- norm1_shift: bfloat16 [1024], P('wsh'), may hold values from -3 to 3
- norm2_gain: bfloat16 [1024], P('wsh'), may hold values from 0.5 to 1.5
- norm2_shift: bfloat16 [1024], P('wsh'), may hold values from -3 to 3
- w_up: bfloat16 [1024, 4096], P('wsh'), may hold values from -0.1875 to 0.1875
- b_up: bfloat16 [4096], P('wsh'), may hold values from -3 to 3
- w_down: bfloat16 [4096, 1024], P('wsh'), may hold values from -0.09375 to 0.09375
- b_down: bfloat16 [1024], P('wsh'), may hold values from -3 to 3
- cotangent: bfloat16 [4, 4096, 1024], P('wsh', 'ctx'), may hold values from -6 to 6
Outputs:
- output: bfloat16 [4, 4096, 1024], P('wsh', 'ctx')
- grad_tokens: bfloat16 [4, 4096, 1024], P('wsh', 'ctx')
- grad_w_qkv: float32 [1024, 3072], P('wsh')
- grad_b_qv: float32 [2048], P('wsh')
- grad_w_out: float32 [1024, 1024], P('wsh')
- grad_b_out: float32 [1024], P('wsh')
- grad_norm1_gain: float32 [1024], P('wsh')
- grad_norm1_shift: float32 [1024], P('wsh')
- grad_norm2_gain: float32 [1024], P('wsh')
- grad_norm2_shift: float32 [1024], P('wsh')
- grad_w_up: float32 [1024, 4096], P('wsh')
- grad_b_up: float32 [4096], P('wsh')
- grad_w_down: float32 [4096, 1024], P('wsh')
- grad_b_down: float32 [1024], P('wsh')
Inputs may be any that keep to these rules, and one draw needn't show every extreme that they name: `places`: within each sequence every position appears once; each device's 128 stored tokens along ctx are two runs of 64 consecutive positions, the run starting at b * 64 followed by the run starting at 4096 - (b + 1) * 64, with b different on every device of the sequence.
All inputs are finite; a program needn't handle non-finite values.
Results may differ from a plain program's by a relative error of at most 0.04.
Values may be sent and summed in bfloat16 or wider, within the bound.
No kernel may reach another device: no remote copies, remote signals or barrier semaphores. Data moves between devices by JAX's collectives and lax.ppermute only.
A program may use at most 192 MiB of HBM per device.

v0:
```python
import functools

import jax
import jax.numpy as jnp
import ml_dtypes
import numpy as np
from jax import lax
from jax.experimental import pallas as pl
from jax.experimental.pallas import tpu as pltpu
from jax.sharding import PartitionSpec as P

HEADS = 16
HEAD_DIM = 64
EPS = 1e-05
NEGATIVE = -1e30
RUN = 64
Q_TILE = 512
K_TILE = 512
F32 = jnp.float32
BF16 = jnp.bfloat16
VMEM = pl.BlockSpec(memory_space=pltpu.VMEM)
SMEM = pl.BlockSpec(memory_space=pltpu.SMEM)
PARAMS = pltpu.CompilerParams(vmem_limit_bytes=20 * 1024 * 1024)
SMALL = pltpu.CompilerParams(vmem_limit_bytes=8 * 1024 * 1024)


def layer_norm(values, gain_vec, shift_vec):
    average = jnp.mean(values, axis=-1, keepdims=True)
    centred = values - average
    variance = jnp.mean(centred * centred, axis=-1, keepdims=True)
    return centred * lax.rsqrt(variance + EPS) * gain_vec + shift_vec


def gelu_tanh(values):
    return (
        0.5
        * values
        * (1.0 + jnp.tanh(0.7978845608028654 * (values + 0.044715 * values * values * values)))
    )


def dot(left, right, left_dim, right_dim):
    return lax.dot_general(
        left, right, (((left_dim,), (right_dim,)), ((), ())), preferred_element_type=F32
    )


VECTORS = (
    (0, 4, 0), (4, 2, 2048), (6, 2, 3072), (8, 2, 4096), (10, 2, 5120), (12, 2, 6144),
    (14, 8, 7168), (22, 2, 11264),
)
MESSAGE_ROWS = RUN + 16


def start_kernel(rank_ref, *refs):
    tokens, (w0, w1, w2a, w2b, w3a, w3b), smalls = refs[:4], refs[4:10], refs[10:14]
    out_ref, normed_ref, weight_ref, vector_ref = refs[14:]
    rank = rank_ref[0]
    for slot, parts in enumerate(((w0,), (w1,), (w2a, w2b), (w3a, w3b))):
        owner = jnp.bitwise_xor(rank, slot)
        size = 256 // len(parts)
        small = smalls[slot][...].astype(F32)
        for i, part in enumerate(parts):
            rows = pl.ds(pl.multiple_of(owner * 256 + i * size, size), size)
            weight_ref[rows, :] = part[...]
        for row, count, base in VECTORS:
            for i in range(count):
                at = pl.multiple_of(base + (owner * count + i) * 128, 128)
                vector_ref[:, pl.ds(at, 128)] = small[row + i : row + i + 1, :]
    gain, shift = vector_ref[:, 3072:4096], vector_ref[:, 4096:5120]
    at = pl.multiple_of(rank * 256, 256)
    biases = (
        vector_ref[:, pl.ds(at, 256)],
        jnp.zeros((1, 256), F32),
        vector_ref[:, pl.ds(pl.multiple_of(1024 + rank * 256, 256), 256)],
    )
    lane = lax.broadcasted_iota(jnp.int32, (16, 384), 1)
    for slot in range(4):
        rows = pl.ds(slot * 128, 128)
        normed = layer_norm(tokens[slot][...].astype(F32), gain, shift).astype(BF16)
        normed_ref[rows, :] = normed
        mixed = dot(normed, weight_ref[...], 1, 0)
        mixed = [mixed[:, part * 256 : part * 256 + 256] + biases[part] for part in range(3)]
        runs = smalls[slot][...].astype(F32)[24:25, :]
        runs = jnp.where(lane % 2 == 0, runs[:, 0:1], runs[:, 1:2]).astype(BF16)
        for head in range(4):
            cols = slice(head * HEAD_DIM, (head + 1) * HEAD_DIM)
            qe, ke, ve = (part[:RUN, cols] for part in mixed)
            ql, kl, vl = (part[RUN:, cols] for part in mixed)
            message = jnp.concatenate([qe, ql, ke, ve, kl, vl], axis=1).astype(BF16)
            out_ref[slot * 4 + head, :RUN, :] = message
            out_ref[slot * 4 + head, RUN:, :] = runs


def start(rank, tokens, weights, smalls):
    args = (rank, *tokens, *weights, *smalls)
    return pl.pallas_call(
        start_kernel,
        out_shape=(
            jax.ShapeDtypeStruct((16, MESSAGE_ROWS, 384), BF16),
            jax.ShapeDtypeStruct((512, 1024), BF16),
            jax.ShapeDtypeStruct((1024, 768), BF16),
            jax.ShapeDtypeStruct((1, 12288), F32),
        ),
        in_specs=[SMEM] + [VMEM] * (len(args) - 1),
        out_specs=(VMEM,) * 4,
        compiler_params=PARAMS,
    )(*args)


def pack_heads_kernel(flat_ref, out_ref):
    for slot in range(4):
        for head in range(4):
            cols = pl.ds(head * HEAD_DIM, HEAD_DIM)
            out_ref[slot * 4 + head] = jnp.concatenate(
                [
                    flat_ref[pl.ds(slot * 128, RUN), cols],
                    flat_ref[pl.ds(slot * 128 + RUN, RUN), cols],
                ],
                axis=1,
            ).astype(BF16)


def pack_heads(flat):
    return pl.pallas_call(
        pack_heads_kernel,
        out_shape=jax.ShapeDtypeStruct((16, RUN, 128), BF16),
        in_specs=[VMEM],
        out_specs=VMEM,
        compiler_params=SMALL,
    )(flat)


def unpack_heads_kernel(packed_ref, out_ref):
    for slot in range(4):
        for half in range(2):
            rows = pl.ds(slot * 128 + half * RUN, RUN)
            out_ref[rows, :] = jnp.concatenate(
                [
                    packed_ref[slot * 4 + head, :, pl.ds(half * HEAD_DIM, HEAD_DIM)]
                    for head in range(4)
                ],
                axis=1,
            )


def unpack_heads(packed):
    return pl.pallas_call(
        unpack_heads_kernel,
        out_shape=jax.ShapeDtypeStruct((512, 256), BF16),
        in_specs=[VMEM],
        out_specs=VMEM,
        compiler_params=SMALL,
    )(packed)


def by_owner(left, right, rank):
    blocks = []
    for slot in range(4):
        at = pl.multiple_of(jnp.bitwise_xor(rank, slot) * 256, 256)
        blocks.append(dot(left[:, pl.ds(at, 256)], right, 0, 0).astype(BF16))
    return blocks


def late_kernel(rank_ref, packed_ref, normed_ref, mixed_ref, out_ref):
    starts = ((0, 128, 192), (64, 256, 320))
    for slot in range(4):
        for half in range(2):
            parts = [[], [], []]
            for head in range(4):
                for part in range(3):
                    lanes = pl.ds(starts[half][part], HEAD_DIM)
                    parts[part].append(packed_ref[slot * 4 + head, :, lanes])
            rows = pl.ds(slot * 128 + half * RUN, RUN)
            mixed_ref[rows, :] = jnp.concatenate(sum(parts, []), axis=1)
    for slot, block in enumerate(by_owner(normed_ref, mixed_ref[...], rank_ref[0])):
        out_ref[:, slot * 16 : slot * 16 + 16, :] = block.reshape(16, 16, 768)


def late_pieces(rank, packed, normed):
    return pl.pallas_call(
        late_kernel,
        out_shape=(
            jax.ShapeDtypeStruct((512, 768), BF16),
            jax.ShapeDtypeStruct((16, 64, 768), BF16),
        ),
        in_specs=[SMEM, VMEM, VMEM],
        out_specs=(VMEM, VMEM),
        compiler_params=PARAMS,
    )(rank, packed, normed)


def early_kernel(
    rank_ref, normed_ref, d_pre_ref, attended_ref, branch_ref, out_ref
):
    for slot, block in enumerate(by_owner(normed_ref, d_pre_ref[...], rank_ref[0])):
        out_ref[:, slot * 16 : slot * 16 + 16, :] = block.reshape(16, 16, 1024)
    block = dot(attended_ref[...], branch_ref[...], 0, 0).astype(BF16)
    out_ref[:, 64:80, :] = block.reshape(16, 16, 1024)


def early_pieces(*args):
    return pl.pallas_call(
        early_kernel,
        out_shape=jax.ShapeDtypeStruct((16, 80, 1024), BF16),
        in_specs=[SMEM] + [VMEM] * 4,
        out_specs=VMEM,
        compiler_params=PARAMS,
    )(*args)


HALF_ROWS = 2048
RANK, ORDER, SORTED = 0, 40, 80
SLOPES = (8.0 * 2.0 ** (-4.0 * (np.arange(HEADS) + 1.0) / HEADS) / 4096.0).astype(np.float32)


def slope_table():
    rest, parts = SLOPES, []
    for _ in range(3):
        parts.append(rest.astype(ml_dtypes.bfloat16).astype(np.float32))
        rest = rest - parts[-1]
    return np.stack(parts, axis=1).reshape(-1)


def sort_runs(runs_ref, sorted_ref, place_ref):
    for place in range(64):
        place_ref[place] = 32
    for source in range(32):
        place_ref[runs_ref[source]] = source

    def step(place, count):
        source = place_ref[place]
        sorted_ref[RANK + source] = count
        sorted_ref[ORDER + count] = place
        return count + (source < 32).astype(jnp.int32)

    lax.fori_loop(0, 64, step, 0)


def run_rows(index):
    return pl.ds(pl.multiple_of(index * RUN, RUN), RUN)


def tile_rows(index, size):
    return pl.ds(pl.multiple_of(index * size, size), size)


def tile_limits(sorted_ref, tile, own):
    per = Q_TILE // RUN
    lane = lax.broadcasted_iota(jnp.int32, (1, Q_TILE), 1)
    if own:
        lowest = tile * Q_TILE
        return lane + lowest, (lowest + 1) // K_TILE, (lowest + Q_TILE - 1) // K_TILE + 1
    counts = [
        (sorted_ref[ORDER + tile * per + i] - (tile * per + i)) * RUN for i in range(per)
    ]
    limits = jnp.zeros((1, Q_TILE), jnp.int32)
    for i in range(per):
        limits = jnp.where(lane // RUN == i, counts[i] - 1, limits)
    return limits, counts[0] // K_TILE, (counts[per - 1] + K_TILE - 1) // K_TILE


def slope_lanes(head_ref, slope_ref):
    lane = lax.broadcasted_iota(jnp.int32, (RUN, HEAD_DIM), 1)
    lanes = jnp.zeros((RUN, HEAD_DIM), F32)
    for i in range(3):
        slope = slope_ref[head_ref[0] * 3 + i]
        lanes = jnp.where(lane == i, slope * RUN, lanes)
        lanes = jnp.where(lane == 3 + i, slope, lanes)
    return lanes.astype(BF16)


def sort_keys(runs_ref, sorted_ref, packed_ref, first_lane, k_ref, v_ref):
    lane = lax.broadcasted_iota(jnp.int32, (RUN, HEAD_DIM), 1)
    offset = lax.broadcasted_iota(jnp.int32, (RUN, HEAD_DIM), 0)
    for source in range(16):
        for half in range(2):
            index = source * 2 + half
            place = run_rows(sorted_ref[RANK + index])
            lanes = jnp.where(lane < 3, runs_ref[index], offset)
            lanes = jnp.where(lane < 6, lanes, 0).astype(F32).astype(BF16)
            at = first_lane + half * 128
            k_ref[place, :] = jnp.concatenate(
                [packed_ref[source, :RUN, pl.ds(at, HEAD_DIM)], lanes], axis=1
            )
            v_ref[place, :] = packed_ref[source, :RUN, pl.ds(at + HEAD_DIM, HEAD_DIM)]


def transpose_rows(source_ref, target_ref):
    for chunk in range(HALF_ROWS // K_TILE):
        rows = pl.ds(chunk * K_TILE, K_TILE)
        target_ref[:, rows] = source_ref[rows, :HEAD_DIM].T


def loop_chunks(step, limits, carry):
    _, full, every = limits
    if isinstance(every, int):
        for chunk in range(every):
            carry = step(chunk >= full, chunk, carry)
        return carry
    carry = lax.fori_loop(0, full, functools.partial(step, False), carry)
    return lax.fori_loop(full, every, functools.partial(step, True), carry)


def masked_scores(masked, chunk, key, query, limits):
    scores = dot(key, query, 1, 1)
    if masked:
        ramp = lax.broadcasted_iota(jnp.int32, (K_TILE, Q_TILE), 0)
        scores = jnp.where(ramp <= limits[0] - chunk * K_TILE, scores, NEGATIVE)
    return scores


def fold_tile(query, limits, carry, k_ref, vt_ref):
    def step(masked, chunk, carry):
        highest, total, accum = carry
        k_rows = tile_rows(chunk, K_TILE)
        scores = masked_scores(masked, chunk, k_ref[k_rows, :], query, limits)
        new_high = jnp.maximum(highest, jnp.max(scores, axis=0, keepdims=True))
        weights = jnp.exp(scores - new_high)
        factor = jnp.exp(highest - new_high)
        total = total * factor + jnp.sum(weights, axis=0, keepdims=True)
        accum = accum * factor + dot(vt_ref[:, k_rows], weights.astype(BF16), 1, 0)
        return new_high, total, accum

    return loop_chunks(step, limits, carry)


def attend_own_kernel(
    head_ref, slope_ref, runs_ref, own_ref,
    sorted_ref, q_ref, k_ref, v_ref, high_ref, total_ref, accum_ref,
    place_ref, vt_ref,
):
    sort_runs(runs_ref, sorted_ref, place_ref)
    lanes = slope_lanes(head_ref, slope_ref)
    for source in range(16):
        for half in range(2):
            query = own_ref[source, :RUN, pl.ds(half * HEAD_DIM, HEAD_DIM)].astype(F32)
            q_ref[run_rows(sorted_ref[RANK + source * 2 + half]), :] = jnp.concatenate(
                [(query * HEAD_DIM ** (-0.5)).astype(BF16), lanes], axis=1
            )
    sort_keys(runs_ref, sorted_ref, own_ref, 128, k_ref, v_ref)
    transpose_rows(v_ref, vt_ref)

    def tile_step(tile, unused):
        q_rows = tile_rows(tile, Q_TILE)
        carry = (
            jnp.full((1, Q_TILE), NEGATIVE, F32),
            jnp.zeros((1, Q_TILE), F32),
            jnp.zeros((HEAD_DIM, Q_TILE), F32),
        )
        limits = tile_limits(sorted_ref, tile, True)
        carry = fold_tile(q_ref[q_rows, :], limits, carry, k_ref, vt_ref)
        high_ref[:, q_rows], total_ref[:, q_rows], accum_ref[:, q_rows] = carry
        return unused

    for tile in range(HALF_ROWS // Q_TILE):
        tile_step(tile, 0)


def attend_other_kernel(
    own_sorted_ref, runs_ref, other_ref, q_ref, high_ref, total_ref, accum_ref,
    out_ref, sorted_ref, k_ref, v_ref, exact_ref, log_ref,
    place_ref, vt_ref, rows_ref,
):
    sort_runs(runs_ref, sorted_ref, place_ref)
    sort_keys(runs_ref, sorted_ref, other_ref, 0, k_ref, v_ref)
    transpose_rows(v_ref, vt_ref)

    def tile_step(tile, unused):
        q_rows = tile_rows(tile, Q_TILE)
        carry = (high_ref[:, q_rows], total_ref[:, q_rows], accum_ref[:, q_rows])
        limits = tile_limits(own_sorted_ref, tile, False)
        highest, total, accum = fold_tile(q_ref[q_rows, :], limits, carry, k_ref, vt_ref)
        exact = accum / total
        exact_ref[:, q_rows] = exact
        log_ref[:, q_rows] = highest + jnp.log(total)
        rows_ref[q_rows, :] = exact.T
        return unused

    lax.fori_loop(0, HALF_ROWS // Q_TILE, tile_step, 0)
    for source in range(16):
        out_ref[source] = jnp.concatenate(
            [rows_ref[run_rows(own_sorted_ref[RANK + source * 2 + half]), :] for half in range(2)],
            axis=1,
        ).astype(BF16)


def unfold_tile(query, d_out, logs, delta, limits, dq, k_ref, v_ref, kt_ref, dk_ref, dv_ref):
    def step(masked, chunk, dq):
        k_rows = tile_rows(chunk, K_TILE)
        scores = masked_scores(masked, chunk, k_ref[k_rows, :], query, limits)
        weights = jnp.exp(scores - logs)
        d_weights = dot(v_ref[k_rows, :], d_out, 1, 1)
        d_scores = (weights * (d_weights - delta)).astype(BF16)
        dv_ref[k_rows, :] += dot(weights.astype(BF16), d_out, 1, 0)
        dk_ref[k_rows, :] += dot(d_scores, query, 1, 0)
        return dq + dot(kt_ref[:, k_rows], d_scores, 1, 0)

    return loop_chunks(step, limits, dq)


def write_keys(sorted_ref, dk_ref, dv_ref, target):
    for source in range(16):
        parts = []
        for half in range(2):
            place = run_rows(sorted_ref[RANK + source * 2 + half])
            parts += [dk_ref[place, :HEAD_DIM], dv_ref[place, :]]
        target[source] = jnp.concatenate(parts, axis=1).astype(target.dtype)


def back_other_kernel(
    own_sorted_ref, sorted_ref, grad_ref, q_ref, k_ref, v_ref, exact_ref, log_ref,
    other_out, dq_ref, do_ref, delta_ref,
    kt_ref, dk_ref, dv_ref,
):
    for source in range(16):
        for half in range(2):
            do_ref[run_rows(own_sorted_ref[RANK + source * 2 + half]), :] = grad_ref[
                source, :, pl.ds(half * HEAD_DIM, HEAD_DIM)
            ]
    transpose_rows(k_ref, kt_ref)
    dk_ref[...] = jnp.zeros_like(dk_ref)
    dv_ref[...] = jnp.zeros_like(dv_ref)

    def tile_step(tile, unused):
        q_rows = tile_rows(tile, Q_TILE)
        d_out = do_ref[q_rows, :]
        delta = jnp.sum(d_out.astype(F32).T * exact_ref[:, q_rows], axis=0, keepdims=True)
        delta_ref[:, q_rows] = delta
        dq_ref[:, q_rows] = unfold_tile(
            q_ref[q_rows, :], d_out, log_ref[:, q_rows], delta,
            tile_limits(own_sorted_ref, tile, False), jnp.zeros((HEAD_DIM, Q_TILE), F32),
            k_ref, v_ref, kt_ref, dk_ref, dv_ref,
        )
        return unused

    lax.fori_loop(0, HALF_ROWS // Q_TILE, tile_step, 0)
    write_keys(sorted_ref, dk_ref, dv_ref, other_out)


def back_own_kernel(
    sorted_ref, do_ref, q_ref, k_ref, v_ref, delta_ref, log_ref, dq_ref,
    dq_out, own_out,
    kt_ref, rows_ref, dk_ref, dv_ref,
):
    transpose_rows(k_ref, kt_ref)
    dk_ref[...] = jnp.zeros_like(dk_ref)
    dv_ref[...] = jnp.zeros_like(dv_ref)

    def tile_step(tile, unused):
        q_rows = tile_rows(tile, Q_TILE)
        dq = unfold_tile(
            q_ref[q_rows, :], do_ref[q_rows, :], log_ref[:, q_rows], delta_ref[:, q_rows],
            tile_limits(sorted_ref, tile, True), dq_ref[:, q_rows],
            k_ref, v_ref, kt_ref, dk_ref, dv_ref,
        )
        rows_ref[q_rows, :] = (dq * HEAD_DIM ** (-0.5)).T
        return unused

    for tile in range(HALF_ROWS // Q_TILE):
        tile_step(tile, 0)
    for source in range(16):
        dq_out[source] = jnp.concatenate(
            [rows_ref[run_rows(sorted_ref[RANK + source * 2 + half]), :] for half in range(2)],
            axis=1,
        ).astype(BF16)
    write_keys(sorted_ref, dk_ref, dv_ref, own_out)


def shape(*dims, dtype=F32):
    return jax.ShapeDtypeStruct(dims, dtype)


def call_attention(kernel, args, outs, scratch, smem):
    return pl.pallas_call(
        kernel,
        out_shape=outs,
        in_specs=[SMEM] * smem + [VMEM] * (len(args) - smem),
        out_specs=tuple(SMEM if out.dtype == jnp.int32 else VMEM for out in outs),
        scratch_shapes=scratch,
        compiler_params=PARAMS,
        cost_estimate=pl.CostEstimate(
            flops=12_000_000_000, bytes_accessed=4_000_000, transcendentals=4_000_000
        ),
    )(*args)


Q_SHAPE = shape(HALF_ROWS, 128, dtype=BF16)
V_SHAPE = shape(HALF_ROWS, HEAD_DIM, dtype=BF16)
ROW_SHAPE = shape(1, HALF_ROWS)
COLUMN_SHAPE = shape(HEAD_DIM, HALF_ROWS)
FLIPPED = pltpu.VMEM((HEAD_DIM, HALF_ROWS), BF16)
NARROW = pltpu.VMEM((HALF_ROWS, HEAD_DIM), F32)
WIDE = pltpu.VMEM((HALF_ROWS, 128), F32)


SORTED_SHAPE = shape(SORTED, dtype=jnp.int32)
PLACES = pltpu.SMEM((64,), jnp.int32)


def attend_own(*args):
    outs = (SORTED_SHAPE, Q_SHAPE, Q_SHAPE, V_SHAPE, ROW_SHAPE, ROW_SHAPE, COLUMN_SHAPE)
    return call_attention(attend_own_kernel, args, outs, [PLACES, FLIPPED], 3)


def attend_other(*args):
    outs = (shape(16, RUN, 128, dtype=BF16), SORTED_SHAPE, Q_SHAPE, V_SHAPE, COLUMN_SHAPE, ROW_SHAPE)
    return call_attention(attend_other_kernel, args, outs, [PLACES, FLIPPED, NARROW], 2)


def back_other(*args):
    outs = (shape(16, RUN, 256, dtype=BF16), COLUMN_SHAPE, V_SHAPE, ROW_SHAPE)
    return call_attention(back_other_kernel, args, outs, [FLIPPED, WIDE, NARROW], 2)


def back_own(*args):
    outs = (shape(16, RUN, 128, dtype=BF16), shape(16, RUN, 256))
    return call_attention(back_own_kernel, args, outs, [FLIPPED, NARROW, WIDE, NARROW], 1)


PLANES = [[2 * i + z for i in range(16)] for z in range(2)]


def swap(value, slot):
    return lax.ppermute(value, "wsh", [(i, i ^ slot) for i in range(4)])


def gather_list(value):
    across = swap(value, 2)
    return [value, swap(value, 1), across, swap(across, 1)]


def gather_slots(value):
    return jnp.concatenate(gather_list(value), axis=0)


def swap_weight(weight, rank, starts, size):
    def columns(slot, row, rows):
        parts = [
            lax.dynamic_slice(
                weight, (row, start + jnp.bitwise_xor(rank, slot) * size), (rows, size)
            )
            for start in starts
        ]
        return jnp.concatenate(parts, axis=1) if len(parts) > 1 else parts[0]

    pieces = [columns(0, 0, 256), columns(1, 0, 256)]
    pieces += [columns(slot, row, 128) for slot in (2, 3) for row in (0, 128)]
    return pieces


def swap_pieces(pieces):
    def wrapped(slot):
        return [(c * 4 + r, (c ^ 1) * 4 + (r ^ slot)) for c in range(32) for r in range(4)]

    return [
        pieces[0], swap(pieces[1], 1),
        swap(pieces[2], 2), lax.ppermute(pieces[3], ("ctx", "wsh"), wrapped(2)),
        swap(pieces[4], 3), lax.ppermute(pieces[5], ("ctx", "wsh"), wrapped(3)),
    ]


def reduce_slots(partial):
    rows = partial.reshape(4, 128, -1)
    across = rows[2] + swap(rows[3].astype(BF16), 1).astype(F32)
    across = swap(across.astype(BF16), 2).astype(F32)
    return rows[0] + swap(rows[1].astype(BF16), 1).astype(F32) + across


def in_order(slots, rank):
    return [
        lax.dynamic_index_in_dim(slots, jnp.bitwise_xor(rank, i), 0, keepdims=False)
        for i in range(4)
    ]


def head_exchange(value):
    return lax.all_to_all(value, "ctx", 0, 0, axis_index_groups=PLANES, tiled=True)


def partner(value):
    return lax.ppermute(value, "ctx", [(i, i ^ 1) for i in range(32)])


def plane_sum(received):
    total = jnp.sum(received.astype(F32), axis=0).astype(BF16)
    return total.astype(F32) + partner(total).astype(F32)


def plane_gather(shard):
    return lax.all_gather(shard, "ctx", axis=0, axis_index_groups=PLANES)


def spread(shard):
    rows = jnp.broadcast_to(shard, (16,) + shard.shape)
    return head_exchange(rows).reshape(rows.shape)


def body(
    tokens,
    places,
    w_qkv,
    b_qv,
    w_out,
    b_out,
    norm1_gain,
    norm1_shift,
    norm2_gain,
    norm2_shift,
    w_up,
    b_up,
    w_down,
    b_down,
    cotangent,
):
    rank = lax.axis_index("wsh")
    column = lax.axis_index("ctx")
    head = rank * 4 + (column // 2) % 4
    rank_scalar = rank.astype(jnp.int32).reshape(1)

    pieces = swap_weight(w_qkv, rank, (0, 1024, 2048), 256)
    vectors = (b_qv, b_out, norm1_gain, norm1_shift, norm2_gain, norm2_shift, b_up, b_down)
    pieces, vectors, places = lax.optimization_barrier((pieces, vectors, places))
    pieces = swap_pieces(pieces)
    runs = (places[0].reshape(2, RUN)[:, 0] // RUN).astype(BF16)
    small = [item.reshape(-1, 128) for item in vectors]
    small = jnp.concatenate(small + [jnp.pad(runs.reshape(1, 2), ((0, 0), (0, 126)))], axis=0)
    smalls = [small] + [swap(small, slot) for slot in (1, 2, 3)]
    smalls, w_up, cotangent = lax.optimization_barrier((smalls, w_up, cotangent))
    packed, normed_one, part_qkv, vector = start(
        rank_scalar, gather_list(tokens[0]), pieces, smalls
    )
    full_bout = vector[0, 2048:3072]
    gain_one = vector[0, 3072:4096]
    shift_one = vector[0, 4096:5120]
    gain_two = vector[0, 5120:6144]
    shift_two = vector[0, 6144:7168]
    bias_up = lax.dynamic_slice_in_dim(vector, 7168 + rank * 1024, 1024, 1)
    full_bdown = vector[0, 11264:]

    own = head_exchange(packed)

    up_pieces = swap_pieces(swap_weight(w_up, rank, (0,), 1024))
    d_down = gather_list(cotangent[0])

    def run_indices(message):
        return message[:, RUN, :2].astype(jnp.int32).reshape(32)

    other = partner(own[:, :, 128:])
    own_sorted, q, k_own, v_own, *state = attend_own(
        head.astype(jnp.int32).reshape(1), slope_table(), run_indices(own), own
    )
    out_packed, other_sorted, k_other, v_other, exact, logs = attend_other(
        own_sorted, run_indices(other), other, q, *state
    )
    out_packed, up_pieces, d_down = lax.optimization_barrier((out_packed, up_pieces, d_down))
    up_slots = [
        up_pieces[0], up_pieces[1],
        jnp.concatenate(up_pieces[2:4], axis=0), jnp.concatenate(up_pieces[4:], axis=0),
    ]
    part_up = jnp.concatenate(in_order(jnp.stack(up_slots), rank), axis=0)
    d_down = jnp.concatenate(d_down, axis=0)
    attended = unpack_heads(head_exchange(out_packed))

    def to_owners(pieces, parts):
        slots = pieces.astype(BF16).reshape(4, 16, -1)
        slots = jnp.stack([slots[0]] + [swap(slots[s], s) for s in (1, 2, 3)])
        return jnp.stack(in_order(slots, rank)).reshape(4, 16, parts, -1)

    residual_in = tokens[0].astype(F32)
    middle = residual_in + reduce_slots(dot(attended, w_out, 1, 0)) + full_bout
    normed_two, norm_two_back = jax.vjp(layer_norm, middle, gain_two, shift_two)
    normed_two = gather_slots(normed_two.astype(BF16))
    pre_act = dot(normed_two, part_up, 1, 0) + bias_up
    hidden, gelu_back = jax.vjp(gelu_tanh, pre_act)
    hidden = hidden.astype(BF16)
    grad_wdown = dot(hidden, d_down, 0, 0).astype(BF16).reshape(16, 64, 1024)

    (d_pre,) = gelu_back(dot(d_down, w_down, 1, 1))
    d_pre, grad_wdown = lax.optimization_barrier((d_pre.astype(BF16), grad_wdown))
    grad_wdown = head_exchange(grad_wdown)
    d_normed_two = reduce_slots(dot(d_pre, part_up, 1, 1))
    d_norm_two, grad_gain_two, grad_shift_two = norm_two_back(d_normed_two)
    d_output = cotangent[0].astype(F32)
    d_middle = d_output + d_norm_two
    d_branch_own = d_middle.astype(BF16)
    d_branch = gather_slots(d_branch_own)
    d_attended = dot(d_branch, w_out, 1, 1)

    d_packed, grad_wdown = lax.optimization_barrier((pack_heads(d_attended), grad_wdown))
    grad = head_exchange(d_packed)
    early = early_pieces(rank_scalar, normed_two, d_pre, attended, d_branch)
    grad, early = lax.optimization_barrier((grad, early))
    early = head_exchange(early)
    grad_wdown = plane_gather(plane_sum(grad_wdown).astype(BF16))
    dkv_other, dq, d_out, delta = back_other(
        own_sorted, other_sorted, grad, q, k_other, v_other, exact, logs
    )
    dkv_other = partner(dkv_other)
    dq, dkv_own = back_own(own_sorted, d_out, q, k_own, v_own, delta, logs, dq)
    dkv = (dkv_own + dkv_other.astype(F32)).astype(BF16)
    d_packed = jnp.concatenate([dq, dkv], axis=2)
    d_packed, early, hidden = lax.optimization_barrier((d_packed, early, hidden))
    d_packed = head_exchange(d_packed)
    output = middle + reduce_slots(dot(hidden, w_down, 1, 0)) + full_bdown
    early = plane_sum(early)
    up_rows = to_owners(early[:64], 1).reshape(64, 1024)
    early = plane_gather(jnp.concatenate([up_rows, early[64:].astype(BF16)], axis=0))
    d_mixed, late = late_pieces(rank_scalar, d_packed, normed_one)
    late = head_exchange(late)
    d_normed_one = reduce_slots(dot(d_mixed, part_qkv, 1, 1))
    _, norm_one_back = jax.vjp(layer_norm, residual_in, gain_one, shift_one)
    d_norm_one, grad_gain_one, grad_shift_one = norm_one_back(d_normed_one)
    grad_input = d_middle + d_norm_one

    sums = jnp.sum(d_mixed.astype(F32), axis=0)
    grad_bqv = jnp.zeros((2048,), F32)
    grad_bqv = lax.dynamic_update_slice_in_dim(grad_bqv, sums[:256], rank * 256, 0)
    grad_bqv = lax.dynamic_update_slice_in_dim(grad_bqv, sums[512:], 1024 + rank * 256, 0)
    grad_bup = lax.dynamic_update_slice_in_dim(
        jnp.zeros((4, 1024), F32), jnp.sum(d_pre.astype(F32), axis=0)[None], rank, 0
    )
    vectors = jnp.concatenate(
        [
            grad_bqv.reshape(4, 512),
            jnp.sum(d_branch_own.astype(F32), axis=0).reshape(4, 256),
            grad_gain_one.reshape(4, 256),
            grad_shift_one.reshape(4, 256),
            grad_gain_two.reshape(4, 256),
            grad_shift_two.reshape(4, 256),
            grad_bup,
            jnp.sum(d_output, axis=0).reshape(4, 256),
        ],
        axis=1,
    )
    vectors = jnp.stack(in_order(vectors, rank)).reshape(4, 24, 128).astype(BF16)
    vectors = vectors.astype(F32) + partner(vectors).astype(F32)
    vector = vectors[0]
    for slot in (1, 2, 3):
        vector = vector + swap(vectors[slot].astype(BF16), slot).astype(F32)
    late, vector = lax.optimization_barrier((late, vector))
    late = to_owners(plane_sum(late), 3).reshape(4, 16, 3, 2, 128)
    late = late.transpose(2, 0, 3, 1, 4).reshape(384, 128)
    late, grad_wdown = lax.optimization_barrier((late, grad_wdown))
    late = spread(jnp.concatenate([late, vector.astype(BF16)], axis=0))

    out_wdown = grad_wdown.reshape(1024, 1024).astype(F32)
    out_wup = early[:, :64].astype(F32).reshape(16, 4, 16, 1024)
    out_wup = out_wup.transpose(0, 2, 1, 3).reshape(256, 4096)
    out_wout = early[:, 64:].astype(F32).reshape(256, 1024)
    out_wqkv = late[:, :384].reshape(16, 24, 16, 128).astype(F32)
    out_wqkv = out_wqkv.transpose(0, 2, 1, 3).reshape(256, 3072)
    out_vec = jnp.sum(late[:, 384:].astype(F32), axis=0).reshape(3072)
    return (
        output.astype(BF16)[None],
        grad_input.astype(BF16)[None],
        out_wqkv,
        out_vec[0:512],
        out_wout,
        out_vec[512:768],
        out_vec[768:1024],
        out_vec[1024:1280],
        out_vec[1280:1536],
        out_vec[1536:1792],
        out_wup,
        out_vec[1792:2816],
        out_wdown,
        out_vec[2816:3072],
    )


def solution(mesh):
    rows = P("wsh", "ctx", None)
    matrix = P("wsh", None)
    vector = P("wsh")
    return jax.shard_map(
        body,
        mesh=mesh,
        in_specs=(
            rows, P("wsh", "ctx"), matrix, vector, matrix, vector, vector, vector, vector, vector,
            matrix, vector, matrix, vector, rows,
        ),
        out_specs=(
            rows, rows, matrix, vector, matrix, vector, vector, vector, vector, vector,
            matrix, vector, matrix, vector,
        ),
        check_vma=False,
    )
```

profile of v0, /device:TPU:0, one launch (start us, length us, event | category | flops | bytes accessed | tf_op | source)
XLA Modules:
  0.0 386.9 jit_solution(7812247865464849241)
XLA Ops:
  13.4 4.0 %collective-permute-start.5 = (bf16[128,768]{1,0:T(8,128)(2,1)}, bf16[128,768]{1,0:T(8,128)(2,1)}, u32[]{:S(2)}, u32[]{:S(2)}) collective-permute-start(bf16[128,768]{1,0:T(8,128)(2,1)} %get-tuple-element.87), channel_id=1, source_target_pairs={{0,6},{1,7},{2,4},{3,5},{4,2},{5,3},{6,0},{7,1},{8,14},{9,15},{10,... | collective-permute-start | bytes 589832 | tf_op jit(solution)/shard_map/ppermute | solution.py:558
  20.3 3.6 collective-permute-done.9.refs_12_
  28.5 6.1 %collective-permute-done.6.refs_8_ = bf16[128,768]{1,0:T(8,128)(2,1)S(1)} collective-permute-done((bf16[128,768]{1,0:T(8,128)(2,1)}, bf16[128,768]{1,0:T(8,128)(2,1)S(1)}, u32[]{:S(2)}, u32[]{:S(2)}) %collective-permute-start.6) | collective-permute-done | bytes 196640 | tf_op jit(solution)/shard_map/ppermute | solution.py:525
  41.7 7.0 %all-to-all-start = ((bf16[16,80,384]{2,1,0:T(8,128)(2,1)}), bf16[16,80,384]{2,1,0:T(8,128)(2,1)S(1)}, u32[]{:S(2)}, u32[]{:S(2)}) async-start(bf16[16,80,384]{2,1,0:T(8,128)(2,1)} %copy-done.14), calls=%async_computation | async-start | bytes 1966080 | tf_op jit(solution)/shard_map/all_to_all | solution.py:578
  54.9 11.2 %all-to-all-done.own_ref = bf16[16,80,384]{2,1,0:T(8,128)(2,1)S(1)} async-done(((bf16[16,80,384]{2,1,0:T(8,128)(2,1)}), bf16[16,80,384]{2,1,0:T(8,128)(2,1)S(1)}, u32[]{:S(2)}, u32[]{:S(2)}) %all-to-all-start) | async-done | bytes 983072 | tf_op jit(solution)/shard_map/all_to_all | solution.py:578
  67.3 6.4 %shard_map.264 = (s32[80]{0:T(128)S(1)}, bf16[2048,128]{1,0:T(8,128)(2,1)S(1)}, bf16[2048,128]{1,0:T(8,128)(2,1)S(1)}, bf16[2048,64]{1,0:T(8,128)(2,1)S(1)}, f32...) custom-call(s32[1]{0:T(128)} %bitcast.1.head_ref, f32[48]{0:T(128)S(1)} %copy-done.17, ...), custom_call_target="tpu_custom_call" | custom-call | flops 12000000000 | bytes 4000000 | tf_op jit(solution)/shard_map/pallas_call | solution.py:475
  76.9 4.8 %collective-permute-done.11.other_ref = bf16[16,80,256]{2,1,0:T(8,128)(2,1)S(1)} collective-permute-done((bf16[16,80,256]{2,1,0:T(8,128)(2,1)S(1)}, bf16[16,80,256]{2,1,0:T(8,128)(2,1)S(1)}, u32[]{:S(2)}, u32[]{:S(2)}) %collective-permute-start.11) | collective-permute-done | bytes 655392 | tf_op jit(solution)/shard_map/ppermute | solution.py:582
  87.8 10.7 %shard_map.265 = (bf16[16,64,128]{2,1,0:T(8,128)(2,1)}, s32[80]{0:T(128)S(1)}, bf16[2048,128]{1,0:T(8,128)(2,1)S(1)}, bf16[2048,64]{1,0:T(8,128)(2,1)S(1)}, f32[...) custom-call(s32[80]{0:T(128)S(1)} %get-tuple-element.104.own_sorted_ref.sorted_ref, s32[32]{0:T(128)S(1)} %reshape.352.runs_ref, ...), custom_call_target="tpu_custom_call" | custom-call | flops 12000000000 | bytes 4000000 | tf_op jit(solution)/shard_map/pallas_call | solution.py:475
  101.0 4.8 %all-to-all-start.1 = ((bf16[16,64,128]{2,1,0:T(8,128)(2,1)}), bf16[16,64,128]{2,1,0:T(8,128)(2,1)S(1)}, u32[]{:S(2)}, u32[]{:S(2)}) async-start(bf16[16,64,128]{2,1,0:T(8,128)(2,1)} %get-tuple-element.112), calls=%async_computation.1 | async-start | bytes 524288 | tf_op jit(solution)/shard_map/all_to_all | solution.py:578
  105.9 9.0 %all-to-all-done.1.packed_ref = bf16[16,64,128]{2,1,0:T(8,128)(2,1)S(1)} async-done(((bf16[16,64,128]{2,1,0:T(8,128)(2,1)}), bf16[16,64,128]{2,1,0:T(8,128)(2,1)S(1)}, u32[]{:S(2)}, u32[]{:S(2)}) %all-to-all-start.1) | async-done | bytes 262176 | tf_op jit(solution)/shard_map/all_to_all | solution.py:578
  122.3 4.7 %collective-permute-done.22 = bf16[128,1024]{1,0:T(8,128)(2,1)S(1)} collective-permute-done((bf16[128,1024]{1,0:T(8,128)(2,1)S(1)}, bf16[128,1024]{1,0:T(8,128)(2,1)S(1)}, u32[]{:S(2)}, u32[]{:S(2)}) %collective-permute-start.22) | collective-permute-done | bytes 262176 | tf_op jit(solution)/shard_map/ppermute | solution.py:525
  129.9 5.6 %collective-permute-done.24 = bf16[128,1024]{1,0:T(8,128)(2,1)S(1)} collective-permute-done((bf16[128,1024]{1,0:T(8,128)(2,1)S(1)}, bf16[128,1024]{1,0:T(8,128)(2,1)S(1)}, u32[]{:S(2)}, u32[]{:S(2)}) %collective-permute-start.24) | collective-permute-done | bytes 262176 | tf_op jit(solution)/shard_map/ppermute | solution.py:525
  148.6 4.4 %all-to-all-start.2 = ((bf16[16,64,1024]{2,1,0:T(8,128)(2,1)}), bf16[16,64,1024]{2,1,0:T(8,128)(2,1)}, u32[]{:S(2)}, u32[]{:S(2)}) async-start(bf16[16,64,1024]{2,1,0:T(8,128)(2,1)} %bitcast.167), calls=%async_computation.2 | async-start | bytes 4194304 | tf_op jit(solution)/shard_map/all_to_all | solution.py:578
  153.0 3.4 collective-permute-done.28
  160.4 6.9 %collective-permute-done.30 = bf16[128,1024]{1,0:T(8,128)(2,1)S(1)} collective-permute-done((bf16[128,1024]{1,0:T(8,128)(2,1)S(1)}, bf16[128,1024]{1,0:T(8,128)(2,1)S(1)}, u32[]{:S(2)}, u32[]{:S(2)}) %collective-permute-start.30) | collective-permute-done | bytes 262176 | tf_op jit(solution)/shard_map/ppermute | solution.py:525
  172.6 11.2 %all-to-all-done.2 = bf16[16,64,1024]{2,1,0:T(8,128)(2,1)} async-done(((bf16[16,64,1024]{2,1,0:T(8,128)(2,1)}), bf16[16,64,1024]{2,1,0:T(8,128)(2,1)}, u32[]{:S(2)}, u32[]{:S(2)}) %all-to-all-start.2) | async-done | bytes 2097184 | tf_op jit(solution)/shard_map/all_to_all | solution.py:578
  183.8 5.0 %all-to-all-start.3 = ((bf16[16,64,128]{2,1,0:T(8,128)(2,1)}), bf16[16,64,128]{2,1,0:T(8,128)(2,1)}, u32[]{:S(2)}, u32[]{:S(2)}) async-start(bf16[16,64,128]{2,1,0:T(8,128)(2,1)} %copy-done.11), calls=%async_computation.3 | async-start | bytes 524288 | tf_op jit(solution)/shard_map/all_to_all | solution.py:578
  199.0 7.2 %all-to-all-start.4 = ((bf16[16,80,1024]{2,1,0:T(8,128)(2,1)}), bf16[16,80,1024]{2,1,0:T(8,128)(2,1)}, u32[]{:S(2)}, u32[]{:S(2)}) async-start(bf16[16,80,1024]{2,1,0:T(8,128)(2,1)} %copy-done.1), calls=%async_computation.4 | async-start | bytes 5242880 | tf_op jit(solution)/shard_map/all_to_all | solution.py:578
  208.5 11.1 %shard_map.269 = (bf16[16,64,256]{2,1,0:T(8,128)(2,1)S(1)}, f32[64,2048]{1,0:T(8,128)S(1)}, bf16[2048,64]{1,0:T(8,128)(2,1)S(1)}, f32[1,2048]{1,0:T(1,128)S(1)}) custom-call(s32[80]{0:T(128)S(1)} %get-tuple-element.104.own_sorted_ref.sorted_ref, s32[80]{0:T(128)S(1)} %get-tuple-element.114.sorted_ref, bf16[16,64,128]{2,1,0:T(8,128)(2,1)} %all-to-all-done.3.grad_ref, ...), custom_call_target="tpu_custom_call" | custom-call | flops 12000000000 | bytes 4000000 | tf_op jit(solution)/shard_map/pallas_call | solution.py:475
  220.6 7.7 %shard_map.270 = (bf16[16,64,128]{2,1,0:T(8,128)(2,1)S(1)}, f32[16,64,256]{2,1,0:T(8,128)S(1)}) custom-call(s32[80]{0:T(128)S(1)} %get-tuple-element.104.own_sorted_ref.sorted_ref, bf16[2048,64]{1,0:T(8,128)(2,1)S(1)} %get-tuple-element.133.do_ref, bf16[2048,128]{1,0:T(8,128)(2,1)S(1)} %copy-done.20, bf16[2048,128]{1,0:T(8,128)(2,1)S(1)} %copy-done.22, ...), custom_call_target="tpu_custom_call" | custom-call | flops 12000000000 | bytes 4000000 | tf_op jit(solution)/shard_map/pallas_call | solution.py:475
  228.3 3.9 %collective-permute-done.32 = bf16[16,64,256]{2,1,0:T(8,128)(2,1)S(1)} collective-permute-done((bf16[16,64,256]{2,1,0:T(8,128)(2,1)S(1)}, bf16[16,64,256]{2,1,0:T(8,128)(2,1)S(1)}, u32[]{:S(2)}, u32[]{:S(2)}) %collective-permute-start.32) | collective-permute-done | bytes 524320 | tf_op jit(solution)/shard_map/ppermute | solution.py:582
  233.4 7.1 %all-to-all-done.4 = bf16[16,80,1024]{2,1,0:T(8,128)(2,1)} async-done(((bf16[16,80,1024]{2,1,0:T(8,128)(2,1)}), bf16[16,80,1024]{2,1,0:T(8,128)(2,1)}, u32[]{:S(2)}, u32[]{:S(2)}) %all-to-all-start.4) | async-done | bytes 2621472 | tf_op jit(solution)/shard_map/all_to_all | solution.py:578
  245.9 4.4 %all-to-all-start.5 = ((bf16[16,64,384]{2,1,0:T(8,128)(2,1)}), bf16[16,64,384]{2,1,0:T(8,128)(2,1)}, u32[]{:S(2)}, u32[]{:S(2)}) async-start(bf16[16,64,384]{2,1,0:T(8,128)(2,1)} %pad_maximum_fusion.4), calls=%async_computation.5 | async-start | bytes 1572864 | tf_op jit(solution)/shard_map/all_to_all | solution.py:578
  269.3 7.0 %all-to-all-start.6 = ((bf16[16,64,768]{2,1,0:T(8,128)(2,1)}), bf16[16,64,768]{2,1,0:T(8,128)(2,1)}, u32[]{:S(2)}, u32[]{:S(2)}) async-start(bf16[16,64,768]{2,1,0:T(8,128)(2,1)} %copy-done.8), calls=%async_computation.6 | async-start | bytes 3145728 | tf_op jit(solution)/shard_map/all_to_all | solution.py:578
  284.1 4.2 %collective-permute-done.38 = bf16[128,1024]{1,0:T(8,128)(2,1)S(1)} collective-permute-done((bf16[128,1024]{1,0:T(8,128)(2,1)}, bf16[128,1024]{1,0:T(8,128)(2,1)S(1)}, u32[]{:S(2)}, u32[]{:S(2)}) %collective-permute-start.38) | collective-permute-done | bytes 262176 | tf_op jit(solution)/shard_map/ppermute | solution.py:525
  301.5 6.1 %all-to-all-done.6 = bf16[16,64,768]{2,1,0:T(8,128)(2,1)} async-done(((bf16[16,64,768]{2,1,0:T(8,128)(2,1)}), bf16[16,64,768]{2,1,0:T(8,128)(2,1)}, u32[]{:S(2)}, u32[]{:S(2)}) %all-to-all-start.6) | async-done | bytes 1572896 | tf_op jit(solution)/shard_map/all_to_all | solution.py:578
  312.5 3.8 fusion.57
  321.9 4.5 %all-to-all-start.7 = ((bf16[16,408,128]{2,1,0:T(8,128)(2,1)}), bf16[16,408,128]{2,1,0:T(8,128)(2,1)}, u32[]{:S(2)}, u32[]{:S(2)}) async-start(bf16[16,408,128]{2,1,0:T(8,128)(2,1)} %broadcast_in_dim.43), calls=%async_computation.7 | async-start | bytes 3342336 | tf_op jit(solution)/shard_map/all_to_all | solution.py:578
  328.8 7.4 %collective-permute-done.35 = bf16[128,1024]{1,0:T(8,128)(2,1)S(1)} collective-permute-done((bf16[128,1024]{1,0:T(8,128)(2,1)S(1)}, bf16[128,1024]{1,0:T(8,128)(2,1)S(1)}, u32[]{:S(2)}, u32[]{:S(2)}) %collective-permute-start.35) | collective-permute-done | bytes 262176 | tf_op jit(solution)/shard_map/ppermute | solution.py:525
  341.9 10.2 %all-to-all-done.7 = bf16[16,408,128]{2,1,0:T(8,128)(2,1)} async-done(((bf16[16,408,128]{2,1,0:T(8,128)(2,1)}), bf16[16,408,128]{2,1,0:T(8,128)(2,1)}, u32[]{:S(2)}, u32[]{:S(2)}) %all-to-all-start.7) | async-done | bytes 1671200 | tf_op jit(solution)/shard_map/all_to_all | solution.py:578
  359.8 6.8 %all-gather.7.cloned.1.call-done = bf16[1280,1024]{1,0:T(8,128)(2,1)} async-done(((bf16[80,1024]{1,0:T(8,128)(2,1)}), bf16[1280,1024]{1,0:T(8,128)(2,1)}) %all-gather.7.cloned.1.call-update) | async-done | bytes 2621456 | tf_op jit(solution)/shard_map/all_gather | solution.py:591
  373.8 5.8 %copy.35 = f32[32,8,4,1024]{3,1,2,0:T(8,128)} copy(f32[32,8,4,1024]{3,2,1,0:T(4,128)S(1)} %bitcast.155) | data formatting | bytes 8388608
  (382 shorter events, 164.8 us)
Async XLA Ops:
  7.2 19.8 %collective-permute-start.1 = (bf16[128,1024]{1,0:T(8,128)(2,1)}, bf16[128,1024]{1,0:T(8,128)(2,1)S(1)}, u32[]{:S(2)}, u32[]{:S(2)}) collective-permute-start(bf16[128,1024]{1,0:T(8,128)(2,1)} %bitcast.152), channel_id=1, source_target_pairs={{0,2},{1,3},{2,0},{3,1},{4,6},{5,7},{6,4},{7,5},{8,10},{9,11},{10,... | collective-permute-start | bytes 786440 | tf_op jit(solution)/shard_map/ppermute | solution.py:525
  13.2 22.7 %collective-permute-start.3 = (bf16[256,768]{1,0:T(8,128)(2,1)}, bf16[256,768]{1,0:T(8,128)(2,1)S(1)}, u32[]{:S(2)}, u32[]{:S(2)}) collective-permute-start(bf16[256,768]{1,0:T(8,128)(2,1)} %get-tuple-element.85), channel_id=1, source_target_pairs={{0,1},{1,0},{2,3},{3,2},{4,5},{5,4},{6,7},{7,6},{8,9},{9,8},{10,11... | collective-permute-start | bytes 1179656 | tf_op jit(solution)/shard_map/ppermute | solution.py:525
  13.2 14.3 %collective-permute-start.4 = (bf16[128,768]{1,0:T(8,128)(2,1)}, bf16[128,768]{1,0:T(8,128)(2,1)}, u32[]{:S(2)}, u32[]{:S(2)}) collective-permute-start(bf16[128,768]{1,0:T(8,128)(2,1)} %get-tuple-element.86), channel_id=1, source_target_pairs={{0,2},{1,3},{2,0},{3,1},{4,6},{5,7},{6,4},{7,5},{8,10},{9,11},{10,... | collective-permute-start | bytes 589832 | tf_op jit(solution)/shard_map/ppermute | solution.py:525
  13.4 14.2 %collective-permute-start.5 = (bf16[128,768]{1,0:T(8,128)(2,1)}, bf16[128,768]{1,0:T(8,128)(2,1)}, u32[]{:S(2)}, u32[]{:S(2)}) collective-permute-start(bf16[128,768]{1,0:T(8,128)(2,1)} %get-tuple-element.87), channel_id=1, source_target_pairs={{0,6},{1,7},{2,4},{3,5},{4,2},{5,3},{6,0},{7,1},{8,14},{9,15},{10,... | collective-permute-start | bytes 589832 | tf_op jit(solution)/shard_map/ppermute | solution.py:558
  27.0 9.0 %collective-permute-start = (bf16[128,1024]{1,0:T(8,128)(2,1)S(1)}, bf16[128,1024]{1,0:T(8,128)(2,1)S(1)}, u32[]{:S(2)}, u32[]{:S(2)}) collective-permute-start(bf16[128,1024]{1,0:T(8,128)(2,1)S(1)} %bitcast.153), channel_id=1, source_target_pairs={{0,1},{1,0},{2,3},{3,2},{4,5},{5,4},{6,7},{7,6},{8,9},{9,8},{10,11... | collective-permute-start | bytes 786440 | tf_op jit(solution)/shard_map/ppermute | solution.py:525
  27.0 9.0 %collective-permute-start.2 = (bf16[128,1024]{1,0:T(8,128)(2,1)S(1)}, bf16[128,1024]{1,0:T(8,128)(2,1)S(1)}, u32[]{:S(2)}, u32[]{:S(2)}) collective-permute-start(bf16[128,1024]{1,0:T(8,128)(2,1)S(1)} %collective-permute-done.1.refs_2_), channel_id=1, source_target_pairs={{0,1},{1,0},{2,3},{3,2},{4,5},{5,4},{6,7},{7,6},{8,9},{9,8},{10,11... | collective-permute-start | bytes 786440 | tf_op jit(solution)/shard_map/ppermute | solution.py:525
  41.7 24.3 %all-to-all-start = ((bf16[16,80,384]{2,1,0:T(8,128)(2,1)}), bf16[16,80,384]{2,1,0:T(8,128)(2,1)S(1)}, u32[]{:S(2)}, u32[]{:S(2)}) async-start(bf16[16,80,384]{2,1,0:T(8,128)(2,1)} %copy-done.14), calls=%async_computation | async-start | bytes 1966080 | tf_op jit(solution)/shard_map/all_to_all | solution.py:578
  48.8 52.1 %collective-permute-start.17 = (bf16[128,1024]{1,0:T(8,128)(2,1)}, bf16[128,1024]{1,0:T(8,128)(2,1)}, u32[]{:S(2)}, u32[]{:S(2)}) collective-permute-start(bf16[128,1024]{1,0:T(8,128)(2,1)} %bitcast.163), channel_id=1, source_target_pairs={{0,1},{1,0},{2,3},{3,2},{4,5},{5,4},{6,7},{7,6},{8,9},{9,8},{10,11... | collective-permute-start | bytes 786440 | tf_op jit(solution)/shard_map/ppermute | solution.py:525
  48.9 35.7 %collective-permute-start.18 = (bf16[128,1024]{1,0:T(8,128)(2,1)}, bf16[128,1024]{1,0:T(8,128)(2,1)}, u32[]{:S(2)}, u32[]{:S(2)}) collective-permute-start(bf16[128,1024]{1,0:T(8,128)(2,1)} %bitcast.164), channel_id=1, source_target_pairs={{0,2},{1,3},{2,0},{3,1},{4,6},{5,7},{6,4},{7,5},{8,10},{9,11},{10,... | collective-permute-start | bytes 786440 | tf_op jit(solution)/shard_map/ppermute | solution.py:525
  51.5 31.2 %collective-permute-start.13 = (bf16[128,1024]{1,0:T(8,128)(2,1)}, bf16[128,1024]{1,0:T(8,128)(2,1)}, u32[]{:S(2)}, u32[]{:S(2)}) collective-permute-start(bf16[128,1024]{1,0:T(8,128)(2,1)} %get-tuple-element.179), channel_id=1, source_target_pairs={{0,2},{1,3},{2,0},{3,1},{4,6},{5,7},{6,4},{7,5},{8,10},{9,11},{10,... | collective-permute-start | bytes 786440 | tf_op jit(solution)/shard_map/ppermute | solution.py:525
  53.2 30.9 %collective-permute-start.14 = (bf16[128,1024]{1,0:T(8,128)(2,1)}, bf16[128,1024]{1,0:T(8,128)(2,1)}, u32[]{:S(2)}, u32[]{:S(2)}) collective-permute-start(bf16[128,1024]{1,0:T(8,128)(2,1)} %get-tuple-element.178), channel_id=1, source_target_pairs={{0,6},{1,7},{2,4},{3,5},{4,2},{5,3},{6,0},{7,1},{8,14},{9,15},{10,... | collective-permute-start | bytes 786440 | tf_op jit(solution)/shard_map/ppermute | solution.py:558
  66.2 15.5 %collective-permute-start.11 = (bf16[16,80,256]{2,1,0:T(8,128)(2,1)S(1)}, bf16[16,80,256]{2,1,0:T(8,128)(2,1)S(1)}, u32[]{:S(2)}, u32[]{:S(2)}) collective-permute-start(bf16[16,80,256]{2,1,0:T(8,128)(2,1)S(1)} %slice.289), channel_id=1, source_target_pairs={{0,4},{4,0},{8,12},{12,8},{16,20},{20,16},{24,28},{28,24},{32,36},... | collective-permute-start | bytes 1966088 | tf_op jit(solution)/shard_map/ppermute | solution.py:582
  81.7 19.3 %collective-permute-start.12 = (bf16[256,1024]{1,0:T(8,128)(2,1)}, bf16[256,1024]{1,0:T(8,128)(2,1)}, u32[]{:S(2)}, u32[]{:S(2)}) collective-permute-start(bf16[256,1024]{1,0:T(8,128)(2,1)} %get-tuple-element.180), channel_id=1, source_target_pairs={{0,1},{1,0},{2,3},{3,2},{4,5},{5,4},{6,7},{7,6},{8,9},{9,8},{10,11... | collective-permute-start | bytes 1572872 | tf_op jit(solution)/shard_map/ppermute | solution.py:525
  82.7 18.3 %collective-permute-start.15 = (bf16[128,1024]{1,0:T(8,128)(2,1)}, bf16[128,1024]{1,0:T(8,128)(2,1)}, u32[]{:S(2)}, u32[]{:S(2)}) collective-permute-start(bf16[128,1024]{1,0:T(8,128)(2,1)} %get-tuple-element.177), channel_id=1, source_target_pairs={{0,3},{1,2},{2,1},{3,0},{4,7},{5,6},{6,5},{7,4},{8,11},{9,10},{10,... | collective-permute-start | bytes 786440 | tf_op jit(solution)/shard_map/ppermute | solution.py:525
  84.1 16.9 %collective-permute-start.16 = (bf16[128,1024]{1,0:T(8,128)(2,1)}, bf16[128,1024]{1,0:T(8,128)(2,1)}, u32[]{:S(2)}, u32[]{:S(2)}) collective-permute-start(bf16[128,1024]{1,0:T(8,128)(2,1)} %get-tuple-element.176), channel_id=1, source_target_pairs={{0,7},{1,6},{2,5},{3,4},{4,3},{5,2},{6,1},{7,0},{8,15},{9,14},{10,... | collective-permute-start | bytes 786440 | tf_op jit(solution)/shard_map/ppermute | solution.py:559
  84.6 16.4 %collective-permute-start.19 = (bf16[128,1024]{1,0:T(8,128)(2,1)}, bf16[128,1024]{1,0:T(8,128)(2,1)}, u32[]{:S(2)}, u32[]{:S(2)}) collective-permute-start(bf16[128,1024]{1,0:T(8,128)(2,1)} %collective-permute-done.18), channel_id=1, source_target_pairs={{0,1},{1,0},{2,3},{3,2},{4,5},{5,4},{6,7},{7,6},{8,9},{9,8},{10,11... | collective-permute-start | bytes 786440 | tf_op jit(solution)/shard_map/ppermute | solution.py:525
  101.0 13.9 %all-to-all-start.1 = ((bf16[16,64,128]{2,1,0:T(8,128)(2,1)}), bf16[16,64,128]{2,1,0:T(8,128)(2,1)S(1)}, u32[]{:S(2)}, u32[]{:S(2)}) async-start(bf16[16,64,128]{2,1,0:T(8,128)(2,1)} %get-tuple-element.112), calls=%async_computation.1 | async-start | bytes 524288 | tf_op jit(solution)/shard_map/all_to_all | solution.py:578
  147.7 8.8 %collective-permute-start.28 = (bf16[128,1024]{1,0:T(8,128)(2,1)}, bf16[128,1024]{1,0:T(8,128)(2,1)S(1)}, u32[]{:S(2)}, u32[]{:S(2)}) collective-permute-start(bf16[128,1024]{1,0:T(8,128)(2,1)} %fusion.22), channel_id=1, source_target_pairs={{0,2},{1,3},{2,0},{3,1},{4,6},{5,7},{6,4},{7,5},{8,10},{9,11},{10,... | collective-permute-start | bytes 786440 | tf_op jit(solution)/shard_map/ppermute | solution.py:525
  148.6 35.2 %all-to-all-start.2 = ((bf16[16,64,1024]{2,1,0:T(8,128)(2,1)}), bf16[16,64,1024]{2,1,0:T(8,128)(2,1)}, u32[]{:S(2)}, u32[]{:S(2)}) async-start(bf16[16,64,1024]{2,1,0:T(8,128)(2,1)} %bitcast.167), calls=%async_computation.2 | async-start | bytes 4194304 | tf_op jit(solution)/shard_map/all_to_all | solution.py:578
  183.8 15.2 %all-to-all-start.3 = ((bf16[16,64,128]{2,1,0:T(8,128)(2,1)}), bf16[16,64,128]{2,1,0:T(8,128)(2,1)}, u32[]{:S(2)}, u32[]{:S(2)}) async-start(bf16[16,64,128]{2,1,0:T(8,128)(2,1)} %copy-done.11), calls=%async_computation.3 | async-start | bytes 524288 | tf_op jit(solution)/shard_map/all_to_all | solution.py:578
  196.3 48.0 %collective-permute-start.47 = (bf16[64,1024]{1,0:T(8,128)(2,1)}, bf16[64,1024]{1,0:T(8,128)(2,1)}, u32[]{:S(2)}, u32[]{:S(2)}) collective-permute-start(bf16[64,1024]{1,0:T(8,128)(2,1)} %reduce_sum.238), channel_id=1, source_target_pairs={{0,4},{4,0},{8,12},{12,8},{16,20},{20,16},{24,28},{28,24},{32,36},... | collective-permute-start | bytes 393224 | tf_op jit(solution)/shard_map/ppermute | solution.py:582
  199.0 41.5 %all-to-all-start.4 = ((bf16[16,80,1024]{2,1,0:T(8,128)(2,1)}), bf16[16,80,1024]{2,1,0:T(8,128)(2,1)}, u32[]{:S(2)}, u32[]{:S(2)}) async-start(bf16[16,80,1024]{2,1,0:T(8,128)(2,1)} %copy-done.1), calls=%async_computation.4 | async-start | bytes 5242880 | tf_op jit(solution)/shard_map/all_to_all | solution.py:578
  206.2 114.3 %all-gather.5.cloned.1.call-start = ((), (), s32[]{:S(2)}) async-start(), calls=%async_computation.8 | async-start | bytes 2228224 | tf_op jit(solution)/shard_map/all_gather | solution.py:591
  219.6 12.6 %collective-permute-start.32 = (bf16[16,64,256]{2,1,0:T(8,128)(2,1)S(1)}, bf16[16,64,256]{2,1,0:T(8,128)(2,1)S(1)}, u32[]{:S(2)}, u32[]{:S(2)}) collective-permute-start(bf16[16,64,256]{2,1,0:T(8,128)(2,1)S(1)} %get-tuple-element.140), channel_id=1, source_target_pairs={{0,4},{4,0},{8,12},{12,8},{16,20},{20,16},{24,28},{28,24},{32,36},... | collective-permute-start | bytes 1572872 | tf_op jit(solution)/shard_map/ppermute | solution.py:582
  245.9 15.9 %all-to-all-start.5 = ((bf16[16,64,384]{2,1,0:T(8,128)(2,1)}), bf16[16,64,384]{2,1,0:T(8,128)(2,1)}, u32[]{:S(2)}, u32[]{:S(2)}) async-start(bf16[16,64,384]{2,1,0:T(8,128)(2,1)} %pad_maximum_fusion.4), calls=%async_computation.5 | async-start | bytes 1572864 | tf_op jit(solution)/shard_map/all_to_all | solution.py:578
  252.3 8.7 %collective-permute-start.51 = (bf16[16,1024]{1,0:T(8,128)(2,1)S(1)}, bf16[16,1024]{1,0:T(8,128)(2,1)}, u32[]{:S(2)}, u32[]{:S(2)}) collective-permute-start(bf16[16,1024]{1,0:T(8,128)(2,1)S(1)} %get-tuple-element.212), channel_id=1, source_target_pairs={{0,3},{1,2},{2,1},{3,0},{4,7},{5,6},{6,5},{7,4},{8,11},{9,10},{10,... | collective-permute-start | bytes 98312 | tf_op jit(solution)/shard_map/ppermute | solution.py:525
  267.9 10.3 %collective-permute-start.37 = (bf16[128,1024]{1,0:T(8,128)(2,1)S(1)}, bf16[128,1024]{1,0:T(8,128)(2,1)S(1)}, u32[]{:S(2)}, u32[]{:S(2)}) collective-permute-start(bf16[128,1024]{1,0:T(8,128)(2,1)S(1)} %get-tuple-element.201), channel_id=1, source_target_pairs={{0,1},{1,0},{2,3},{3,2},{4,5},{5,4},{6,7},{7,6},{8,9},{9,8},{10,11... | collective-permute-start | bytes 786440 | tf_op jit(solution)/shard_map/ppermute | solution.py:525
  268.8 15.3 %collective-permute-start.36 = (bf16[128,1024]{1,0:T(8,128)(2,1)S(1)}, bf16[128,1024]{1,0:T(8,128)(2,1)S(1)}, u32[]{:S(2)}, u32[]{:S(2)}) collective-permute-start(bf16[128,1024]{1,0:T(8,128)(2,1)S(1)} %get-tuple-element.200), channel_id=1, source_target_pairs={{0,1},{1,0},{2,3},{3,2},{4,5},{5,4},{6,7},{7,6},{8,9},{9,8},{10,11... | collective-permute-start | bytes 786440 | tf_op jit(solution)/shard_map/ppermute | solution.py:525
  269.3 38.4 %all-to-all-start.6 = ((bf16[16,64,768]{2,1,0:T(8,128)(2,1)}), bf16[16,64,768]{2,1,0:T(8,128)(2,1)}, u32[]{:S(2)}, u32[]{:S(2)}) async-start(bf16[16,64,768]{2,1,0:T(8,128)(2,1)} %copy-done.8), calls=%async_computation.6 | async-start | bytes 3145728 | tf_op jit(solution)/shard_map/all_to_all | solution.py:578
  276.2 90.4 %all-gather.7.cloned.1.call-start = ((), (), s32[]{:S(2)}) async-start(), calls=%async_computation.9 | async-start | bytes 2785280 | tf_op jit(solution)/shard_map/all_gather | solution.py:591
  319.1 9.7 %collective-permute-start.33 = (bf16[128,1024]{1,0:T(8,128)(2,1)}, bf16[128,1024]{1,0:T(8,128)(2,1)}, u32[]{:S(2)}, u32[]{:S(2)}) collective-permute-start(bf16[128,1024]{1,0:T(8,128)(2,1)} %get-tuple-element.202), channel_id=1, source_target_pairs={{0,1},{1,0},{2,3},{3,2},{4,5},{5,4},{6,7},{7,6},{8,9},{9,8},{10,11... | collective-permute-start | bytes 786440 | tf_op jit(solution)/shard_map/ppermute | solution.py:525
  321.9 30.2 %all-to-all-start.7 = ((bf16[16,408,128]{2,1,0:T(8,128)(2,1)}), bf16[16,408,128]{2,1,0:T(8,128)(2,1)}, u32[]{:S(2)}, u32[]{:S(2)}) async-start(bf16[16,408,128]{2,1,0:T(8,128)(2,1)} %broadcast_in_dim.43), calls=%async_computation.7 | async-start | bytes 3342336 | tf_op jit(solution)/shard_map/all_to_all | solution.py:578
  (106 other events, 781.8 us)
Sparse Core Ops, SparseCore 0:
  246.1 59.4 all-gather.4
  307.8 58.7 all-gather.6
where the time goes:
time: 394 us; the launch traced here: 387 us
  waiting for transfers between devices  125 us (32%)
  starting transfers between devices  82.2 us (21%)
  local copies, waits for them, and re-layouts  62.2 us (16%)
  Pallas kernels  42.8 us (11%)
  other arithmetic  42.5 us (11%)
  matrix products  16.2 us (4%)
  between operations  15.9 us (4%)
    all_to_all x8, waiting for transfers between devices, head_exchange(): lax.all_to_all(value, 'ctx', 0, 0, axis_index_groups=PLANES, tiled=True)  54.8 us
    ppermute x42, waiting for transfers between devices, swap(): return lax.ppermute(value, 'wsh', [(i, i ^ slot) for i in range(4)])  51.2 us
    all_to_all x8, starting transfers between devices, head_exchange(): lax.all_to_all(value, 'ctx', 0, 0, axis_index_groups=PLANES, tiled=True)  44.3 us
    pallas_call x4, Pallas kernels, call_attention(): pl.pallas_call(kernel, out_shape=outs, in_specs=[SMEM] * smem + [VMEM] *...  35.9 us
    unnamed x165, local copies, waits for them, and re-layouts  31.2 us
    ppermute x42, starting transfers between devices, swap(): return lax.ppermute(value, 'wsh', [(i, i ^ slot) for i in range(4)])  20 us
    dot_general x8, matrix products, dot(): lax.dot_general(left, right, (((left_dim,), (right_dim,)), ((), ())), pre...  16.2 us
    ppermute x6, starting transfers between devices, partner(): return lax.ppermute(value, 'ctx', [(i, i ^ 1) for i in range(32)])  11.4 us
  transfers between devices with their start and end apart: 62, of which 28 were waited for; matrix products, arithmetic and copies ran while one was open for 20% of the time, Pallas kernels for 10%

commit v1 on v0

--- a/solution.py
+++ b/solution.py
@@ -209,6 +209,50 @@
     )(*args)
 
 
+def spread_early_kernel(packed_ref, up_ref, out_ref):
+    for piece in range(16):
+        rows = slice(piece * 16, piece * 16 + 16)
+        for block in range(4):
+            up_ref[rows, block * 1024 : block * 1024 + 1024] = packed_ref[
+                piece, block * 16 : block * 16 + 16, :
+            ].astype(F32)
+        out_ref[rows, :] = packed_ref[piece, 64:80, :].astype(F32)
+
+
+def spread_early(packed):
+    return pl.pallas_call(
+        spread_early_kernel,
+        out_shape=(
+            jax.ShapeDtypeStruct((256, 4096), F32), jax.ShapeDtypeStruct((256, 1024), F32)
+        ),
+        in_specs=[VMEM],
+        out_specs=(VMEM, VMEM),
+        compiler_params=PARAMS,
+    )(packed)
+
+
+def spread_late_kernel(packed_ref, qkv_ref, vector_ref):
+    for piece in range(16):
+        rows = slice(piece * 16, piece * 16 + 16)
+        for block in range(24):
+            qkv_ref[rows, block * 128 : block * 128 + 128] = packed_ref[
+                piece, block * 16 : block * 16 + 16, :
+            ].astype(F32)
+    vector_ref[...] = jnp.sum(packed_ref[:, 384:, :].astype(F32), axis=0)
+
+
+def spread_late(packed):
+    return pl.pallas_call(
+        spread_late_kernel,
+        out_shape=(
+            jax.ShapeDtypeStruct((256, 3072), F32), jax.ShapeDtypeStruct((32, 128), F32)
+        ),
+        in_specs=[VMEM],
+        out_specs=(VMEM, VMEM),
+        compiler_params=PARAMS,
+    )(packed)
+
+
 HALF_ROWS = 2048
 RANK, ORDER, SORTED = 0, 40, 80
 SLOPES = (8.0 * 2.0 ** (-4.0 * (np.arange(HEADS) + 1.0) / HEADS) / 4096.0).astype(np.float32)
@@ -665,7 +709,8 @@
     def to_owners(pieces, parts):
         slots = pieces.astype(BF16).reshape(4, 16, -1)
         slots = jnp.stack([slots[0]] + [swap(slots[s], s) for s in (1, 2, 3)])
-        return jnp.stack(in_order(slots, rank)).reshape(4, 16, parts, -1)
+        columns = jnp.stack(in_order(slots, rank))
+        return columns if parts == 1 else columns.reshape(4, 16, parts, -1)
 
     residual_in = tokens[0].astype(F32)
     middle = residual_in + reduce_slots(dot(attended, w_out, 1, 0)) + full_bout
@@ -742,15 +787,13 @@
     late = to_owners(plane_sum(late), 3).reshape(4, 16, 3, 2, 128)
     late = late.transpose(2, 0, 3, 1, 4).reshape(384, 128)
     late, grad_wdown = lax.optimization_barrier((late, grad_wdown))
-    late = spread(jnp.concatenate([late, vector.astype(BF16)], axis=0))
+    vector = jnp.pad(vector.astype(BF16), ((0, 8), (0, 0)))
+    late = spread(jnp.concatenate([late, vector], axis=0))
 
     out_wdown = grad_wdown.reshape(1024, 1024).astype(F32)
-    out_wup = early[:, :64].astype(F32).reshape(16, 4, 16, 1024)
-    out_wup = out_wup.transpose(0, 2, 1, 3).reshape(256, 4096)
-    out_wout = early[:, 64:].astype(F32).reshape(256, 1024)
-    out_wqkv = late[:, :384].reshape(16, 24, 16, 128).astype(F32)
-    out_wqkv = out_wqkv.transpose(0, 2, 1, 3).reshape(256, 3072)
-    out_vec = jnp.sum(late[:, 384:].astype(F32), axis=0).reshape(3072)
+    out_wup, out_wout = spread_early(early)
+    out_wqkv, out_vec = spread_late(late)
+    out_vec = out_vec[:24].reshape(3072)
     return (
         output.astype(BF16)[None],
         grad_input.astype(BF16)[None],

time: 394 us -> 378 us (0.959)
  local copies, waits for them, and re-layouts: 62.2 us -> 43.2 us
  Pallas kernels: 42.8 us -> 48.8 us
  other arithmetic: 42.5 us -> 37 us
    unnamed x165 -> x155, local copies, waits for them, and re-layouts: 31.2 us -> 24.2 us
    all_gather x2, waiting for transfers between devices: 6.78 us -> 0.02 us  [plane_gather(): return lax.all_gather(shard, 'ctx', axis=0, axis_index_groups=PLANES)]
    pallas_call x0 -> x2, Pallas kernels: none -> 6 us  [the longest x1 3.32 us: spread_late(): pl.pallas_call(spread_late_kernel, out_shape=(jax.ShapeDtypeStruct((256,...]
    all_to_all x8, waiting for transfers between devices: 54.8 us -> 60.7 us  [head_exchange(): lax.all_to_all(value, 'ctx', 0, 0, axis_index_groups=PLANES, tiled=True)]
    slice x3 -> x0, local copies, waits for them, and re-layouts: 4.36 us -> none  [the longest x1 1.77 us: body(): out_wup = early[:, :64].astype(F32).reshape(16, 4, 16, 1024)]
  transfers between devices with their start and end apart: 62 -> 62, of which waited for: 28 -> 28; matrix products, arithmetic and copies ran while one was open for 20% -> 18% of each run, Pallas kernels for 10% -> 12%
where the time goes in v1:
time: 378 us; the launch traced here: 371 us
  waiting for transfers between devices  127 us (34%)
  starting transfers between devices  83.1 us (22%)
  Pallas kernels  48.8 us (13%)
  local copies, waits for them, and re-layouts  43.2 us (11%)
  other arithmetic  37 us (10%)
  matrix products  16.2 us (4%)
  between operations  15.8 us (4%)
    all_to_all x8, waiting for transfers between devices, head_exchange(): lax.all_to_all(value, 'ctx', 0, 0, axis_index_groups=PLANES, tiled=True)  60.7 us
    ppermute x42, waiting for transfers between devices, swap(): return lax.ppermute(value, 'wsh', [(i, i ^ slot) for i in range(4)])  53.4 us
    all_to_all x8, starting transfers between devices, head_exchange(): lax.all_to_all(value, 'ctx', 0, 0, axis_index_groups=PLANES, tiled=True)  42.5 us
    pallas_call x4, Pallas kernels, call_attention(): pl.pallas_call(kernel, out_shape=outs, in_specs=[SMEM] * smem + [VMEM] *...  35.9 us
    unnamed x155, local copies, waits for them, and re-layouts  24.2 us
    ppermute x42, starting transfers between devices, swap(): return lax.ppermute(value, 'wsh', [(i, i ^ slot) for i in range(4)])  20 us
    dot_general x8, matrix products, dot(): lax.dot_general(left, right, (((left_dim,), (right_dim,)), ((), ())), pre...  16.2 us
    ppermute x6, starting transfers between devices, partner(): return lax.ppermute(value, 'ctx', [(i, i ^ 1) for i in range(32)])  14.4 us
  transfers between devices with their start and end apart: 62, of which 28 were waited for; matrix products, arithmetic and copies ran while one was open for 18% of the time, Pallas kernels for 12%

profile of v1, /device:TPU:0, one launch (start us, length us, event | category | flops | bytes accessed | tf_op | source)
XLA Modules:
  0.0 370.8 jit_solution(348807351530455424)
XLA Ops:
  13.4 4.0 %collective-permute-start.5 = (bf16[128,768]{1,0:T(8,128)(2,1)}, bf16[128,768]{1,0:T(8,128)(2,1)}, u32[]{:S(2)}, u32[]{:S(2)}) collective-permute-start(bf16[128,768]{1,0:T(8,128)(2,1)} %get-tuple-element.91), channel_id=1, source_target_pairs={{0,6},{1,7},{2,4},{3,5},{4,2},{5,3},{6,0},{7,1},{8,14},{9,15},{10,... | collective-permute-start | bytes 589832 | tf_op jit(solution)/shard_map/ppermute | solution.py:602
  20.3 3.6 collective-permute-done.9.refs_12_
  28.5 6.1 %collective-permute-done.6.refs_8_ = bf16[128,768]{1,0:T(8,128)(2,1)S(1)} collective-permute-done((bf16[128,768]{1,0:T(8,128)(2,1)}, bf16[128,768]{1,0:T(8,128)(2,1)S(1)}, u32[]{:S(2)}, u32[]{:S(2)}) %collective-permute-start.6) | collective-permute-done | bytes 196640 | tf_op jit(solution)/shard_map/ppermute | solution.py:569
  41.7 7.0 %all-to-all-start = ((bf16[16,80,384]{2,1,0:T(8,128)(2,1)}), bf16[16,80,384]{2,1,0:T(8,128)(2,1)S(1)}, u32[]{:S(2)}, u32[]{:S(2)}) async-start(bf16[16,80,384]{2,1,0:T(8,128)(2,1)} %copy-done.15), calls=%async_computation | async-start | bytes 1966080 | tf_op jit(solution)/shard_map/all_to_all | solution.py:622
  54.9 11.2 %all-to-all-done.own_ref = bf16[16,80,384]{2,1,0:T(8,128)(2,1)S(1)} async-done(((bf16[16,80,384]{2,1,0:T(8,128)(2,1)}), bf16[16,80,384]{2,1,0:T(8,128)(2,1)S(1)}, u32[]{:S(2)}, u32[]{:S(2)}) %all-to-all-start) | async-done | bytes 983072 | tf_op jit(solution)/shard_map/all_to_all | solution.py:622
  67.6 6.4 %shard_map.264 = (s32[80]{0:T(128)S(1)}, bf16[2048,128]{1,0:T(8,128)(2,1)S(1)}, bf16[2048,128]{1,0:T(8,128)(2,1)S(1)}, bf16[2048,64]{1,0:T(8,128)(2,1)S(1)}, f32...) custom-call(s32[1]{0:T(128)} %bitcast.1.head_ref, f32[48]{0:T(128)S(1)} %copy-done.18, ...), custom_call_target="tpu_custom_call" | custom-call | flops 12000000000 | bytes 4000000 | tf_op jit(solution)/shard_map/pallas_call | solution.py:519
  77.1 4.8 %collective-permute-done.11.other_ref = bf16[16,80,256]{2,1,0:T(8,128)(2,1)S(1)} collective-permute-done((bf16[16,80,256]{2,1,0:T(8,128)(2,1)S(1)}, bf16[16,80,256]{2,1,0:T(8,128)(2,1)S(1)}, u32[]{:S(2)}, u32[]{:S(2)}) %collective-permute-start.11) | collective-permute-done | bytes 655392 | tf_op jit(solution)/shard_map/ppermute | solution.py:626
  88.0 10.8 %shard_map.265 = (bf16[16,64,128]{2,1,0:T(8,128)(2,1)}, s32[80]{0:T(128)S(1)}, bf16[2048,128]{1,0:T(8,128)(2,1)S(1)}, bf16[2048,64]{1,0:T(8,128)(2,1)S(1)}, f32[...) custom-call(s32[80]{0:T(128)S(1)} %get-tuple-element.108.own_sorted_ref.sorted_ref, s32[32]{0:T(128)S(1)} %reshape.324.runs_ref, ...), custom_call_target="tpu_custom_call" | custom-call | flops 12000000000 | bytes 4000000 | tf_op jit(solution)/shard_map/pallas_call | solution.py:519
  101.3 4.8 %all-to-all-start.1 = ((bf16[16,64,128]{2,1,0:T(8,128)(2,1)}), bf16[16,64,128]{2,1,0:T(8,128)(2,1)S(1)}, u32[]{:S(2)}, u32[]{:S(2)}) async-start(bf16[16,64,128]{2,1,0:T(8,128)(2,1)} %get-tuple-element.116), calls=%async_computation.1 | async-start | bytes 524288 | tf_op jit(solution)/shard_map/all_to_all | solution.py:622
  106.1 9.0 %all-to-all-done.1.packed_ref = bf16[16,64,128]{2,1,0:T(8,128)(2,1)S(1)} async-done(((bf16[16,64,128]{2,1,0:T(8,128)(2,1)}), bf16[16,64,128]{2,1,0:T(8,128)(2,1)S(1)}, u32[]{:S(2)}, u32[]{:S(2)}) %all-to-all-start.1) | async-done | bytes 262176 | tf_op jit(solution)/shard_map/all_to_all | solution.py:622
  122.7 4.5 %collective-permute-done.22 = bf16[128,1024]{1,0:T(8,128)(2,1)S(1)} collective-permute-done((bf16[128,1024]{1,0:T(8,128)(2,1)S(1)}, bf16[128,1024]{1,0:T(8,128)(2,1)S(1)}, u32[]{:S(2)}, u32[]{:S(2)}) %collective-permute-start.22) | collective-permute-done | bytes 262176 | tf_op jit(solution)/shard_map/ppermute | solution.py:569
  130.3 5.4 %collective-permute-done.24 = bf16[128,1024]{1,0:T(8,128)(2,1)S(1)} collective-permute-done((bf16[128,1024]{1,0:T(8,128)(2,1)S(1)}, bf16[128,1024]{1,0:T(8,128)(2,1)S(1)}, u32[]{:S(2)}, u32[]{:S(2)}) %collective-permute-start.24) | collective-permute-done | bytes 262176 | tf_op jit(solution)/shard_map/ppermute | solution.py:569
  148.6 4.4 %all-to-all-start.2 = ((bf16[16,64,1024]{2,1,0:T(8,128)(2,1)}), bf16[16,64,1024]{2,1,0:T(8,128)(2,1)}, u32[]{:S(2)}, u32[]{:S(2)}) async-start(bf16[16,64,1024]{2,1,0:T(8,128)(2,1)} %bitcast.141), calls=%async_computation.2 | async-start | bytes 4194304 | tf_op jit(solution)/shard_map/all_to_all | solution.py:622
  153.1 3.4 collective-permute-done.28
  160.4 6.9 %collective-permute-done.30 = bf16[128,1024]{1,0:T(8,128)(2,1)S(1)} collective-permute-done((bf16[128,1024]{1,0:T(8,128)(2,1)S(1)}, bf16[128,1024]{1,0:T(8,128)(2,1)S(1)}, u32[]{:S(2)}, u32[]{:S(2)}) %collective-permute-start.30) | collective-permute-done | bytes 262176 | tf_op jit(solution)/shard_map/ppermute | solution.py:569
  172.6 11.3 %all-to-all-done.2 = bf16[16,64,1024]{2,1,0:T(8,128)(2,1)} async-done(((bf16[16,64,1024]{2,1,0:T(8,128)(2,1)}), bf16[16,64,1024]{2,1,0:T(8,128)(2,1)}, u32[]{:S(2)}, u32[]{:S(2)}) %all-to-all-start.2) | async-done | bytes 2097184 | tf_op jit(solution)/shard_map/all_to_all | solution.py:622
  183.9 5.0 %all-to-all-start.3 = ((bf16[16,64,128]{2,1,0:T(8,128)(2,1)}), bf16[16,64,128]{2,1,0:T(8,128)(2,1)}, u32[]{:S(2)}, u32[]{:S(2)}) async-start(bf16[16,64,128]{2,1,0:T(8,128)(2,1)} %copy-done.12), calls=%async_computation.3 | async-start | bytes 524288 | tf_op jit(solution)/shard_map/all_to_all | solution.py:622
  199.5 7.6 %all-to-all-start.4 = ((bf16[16,80,1024]{2,1,0:T(8,128)(2,1)}), bf16[16,80,1024]{2,1,0:T(8,128)(2,1)}, u32[]{:S(2)}, u32[]{:S(2)}) async-start(bf16[16,80,1024]{2,1,0:T(8,128)(2,1)} %copy-done.1), calls=%async_computation.4 | async-start | bytes 5242880 | tf_op jit(solution)/shard_map/all_to_all | solution.py:622
  209.2 11.1 %shard_map.269 = (bf16[16,64,256]{2,1,0:T(8,128)(2,1)S(1)}, f32[64,2048]{1,0:T(8,128)S(1)}, bf16[2048,64]{1,0:T(8,128)(2,1)S(1)}, f32[1,2048]{1,0:T(1,128)S(1)}) custom-call(s32[80]{0:T(128)S(1)} %get-tuple-element.108.own_sorted_ref.sorted_ref, s32[80]{0:T(128)S(1)} %get-tuple-element.118.sorted_ref, bf16[16,64,128]{2,1,0:T(8,128)(2,1)} %all-to-all-done.3.grad_ref, ...), custom_call_target="tpu_custom_call" | custom-call | flops 12000000000 | bytes 4000000 | tf_op jit(solution)/shard_map/pallas_call | solution.py:519
  222.7 7.7 %shard_map.270 = (bf16[16,64,128]{2,1,0:T(8,128)(2,1)S(1)}, f32[16,64,256]{2,1,0:T(8,128)S(1)}) custom-call(s32[80]{0:T(128)S(1)} %get-tuple-element.108.own_sorted_ref.sorted_ref, bf16[2048,64]{1,0:T(8,128)(2,1)S(1)} %get-tuple-element.137.do_ref, bf16[2048,128]{1,0:T(8,128)(2,1)S(1)} %copy-done.21, bf16[2048,128]{1,0:T(8,128)(2,1)S(1)} %copy-done.23, ...), custom_call_target="tpu_custom_call" | custom-call | flops 12000000000 | bytes 4000000 | tf_op jit(solution)/shard_map/pallas_call | solution.py:519
  230.4 3.4 collective-permute-done.32
  234.9 8.6 %all-to-all-done.4 = bf16[16,80,1024]{2,1,0:T(8,128)(2,1)} async-done(((bf16[16,80,1024]{2,1,0:T(8,128)(2,1)}), bf16[16,80,1024]{2,1,0:T(8,128)(2,1)}, u32[]{:S(2)}, u32[]{:S(2)}) %all-to-all-start.4) | async-done | bytes 2621472 | tf_op jit(solution)/shard_map/all_to_all | solution.py:622
  248.4 4.3 %all-to-all-start.5 = ((bf16[16,64,384]{2,1,0:T(8,128)(2,1)}), bf16[16,64,384]{2,1,0:T(8,128)(2,1)}, u32[]{:S(2)}, u32[]{:S(2)}) async-start(bf16[16,64,384]{2,1,0:T(8,128)(2,1)} %pad_maximum_fusion.4), calls=%async_computation.5 | async-start | bytes 1572864 | tf_op jit(solution)/shard_map/all_to_all | solution.py:622
  265.5 4.3 %all-to-all-done.5.packed_ref = bf16[16,64,384]{2,1,0:T(8,128)(2,1)} async-done(((bf16[16,64,384]{2,1,0:T(8,128)(2,1)}), bf16[16,64,384]{2,1,0:T(8,128)(2,1)}, u32[]{:S(2)}, u32[]{:S(2)}) %all-to-all-start.5) | async-done | bytes 786464 | tf_op jit(solution)/shard_map/all_to_all | solution.py:622
  276.8 4.8 %all-to-all-start.6 = ((bf16[16,64,768]{2,1,0:T(8,128)(2,1)}), bf16[16,64,768]{2,1,0:T(8,128)(2,1)}, u32[]{:S(2)}, u32[]{:S(2)}) async-start(bf16[16,64,768]{2,1,0:T(8,128)(2,1)} %copy-done.9), calls=%async_computation.6 | async-start | bytes 3145728 | tf_op jit(solution)/shard_map/all_to_all | solution.py:622
  285.0 6.7 %collective-permute-done.38 = bf16[128,1024]{1,0:T(8,128)(2,1)S(1)} collective-permute-done((bf16[128,1024]{1,0:T(8,128)(2,1)}, bf16[128,1024]{1,0:T(8,128)(2,1)S(1)}, u32[]{:S(2)}, u32[]{:S(2)}) %collective-permute-start.38) | collective-permute-done | bytes 262176 | tf_op jit(solution)/shard_map/ppermute | solution.py:569
  303.7 5.2 %all-to-all-done.6 = bf16[16,64,768]{2,1,0:T(8,128)(2,1)} async-done(((bf16[16,64,768]{2,1,0:T(8,128)(2,1)}), bf16[16,64,768]{2,1,0:T(8,128)(2,1)}, u32[]{:S(2)}, u32[]{:S(2)}) %all-to-all-start.6) | async-done | bytes 1572896 | tf_op jit(solution)/shard_map/all_to_all | solution.py:622
  313.6 3.8 %fusion.59 = (bf16[512,1024]{1,0:T(8,128)(2,1)S(1)}, f32[512,1024]{1,0:T(8,128)}) fusion(bf16[512,1024]{1,0:T(8,128)(2,1)} %copy-done.71, bf16[1024,1024]{1,0:T(8,128)(2,1)S(1)} %copy-done), kind=kOutput, calls=%fused_computation.196 | convolution fusion | flops 1074266112 | bytes 6291456 | tf_op jit(solution)/shard_map/dot_general | solution.py:43
  323.1 4.6 %all-to-all-start.7 = ((bf16[16,416,128]{2,1,0:T(8,128)(2,1)}), bf16[16,416,128]{2,1,0:T(8,128)(2,1)}, u32[]{:S(2)}, u32[]{:S(2)}) async-start(bf16[16,416,128]{2,1,0:T(8,128)(2,1)} %broadcast_in_dim.43), calls=%async_computation.7 | async-start | bytes 3407872 | tf_op jit(solution)/shard_map/all_to_all | solution.py:622
  329.7 7.5 %collective-permute-done.35 = bf16[128,1024]{1,0:T(8,128)(2,1)S(1)} collective-permute-done((bf16[128,1024]{1,0:T(8,128)(2,1)S(1)}, bf16[128,1024]{1,0:T(8,128)(2,1)S(1)}, u32[]{:S(2)}, u32[]{:S(2)}) %collective-permute-start.35) | collective-permute-done | bytes 262176 | tf_op jit(solution)/shard_map/ppermute | solution.py:569
  342.9 11.1 %all-to-all-done.7.packed_ref = bf16[16,416,128]{2,1,0:T(8,128)(2,1)} async-done(((bf16[16,416,128]{2,1,0:T(8,128)(2,1)}), bf16[16,416,128]{2,1,0:T(8,128)(2,1)}, u32[]{:S(2)}, u32[]{:S(2)}) %all-to-all-start.7) | async-done | bytes 1703968 | tf_op jit(solution)/shard_map/all_to_all | solution.py:622
  354.0 3.3 shard_map.272
  (365 shorter events, 152.3 us)
Async XLA Ops:
  7.2 19.8 %collective-permute-start.1 = (bf16[128,1024]{1,0:T(8,128)(2,1)}, bf16[128,1024]{1,0:T(8,128)(2,1)S(1)}, u32[]{:S(2)}, u32[]{:S(2)}) collective-permute-start(bf16[128,1024]{1,0:T(8,128)(2,1)} %bitcast.133), channel_id=1, source_target_pairs={{0,2},{1,3},{2,0},{3,1},{4,6},{5,7},{6,4},{7,5},{8,10},{9,11},{10,... | collective-permute-start | bytes 786440 | tf_op jit(solution)/shard_map/ppermute | solution.py:569
  13.2 22.7 %collective-permute-start.3 = (bf16[256,768]{1,0:T(8,128)(2,1)}, bf16[256,768]{1,0:T(8,128)(2,1)S(1)}, u32[]{:S(2)}, u32[]{:S(2)}) collective-permute-start(bf16[256,768]{1,0:T(8,128)(2,1)} %get-tuple-element.89), channel_id=1, source_target_pairs={{0,1},{1,0},{2,3},{3,2},{4,5},{5,4},{6,7},{7,6},{8,9},{9,8},{10,11... | collective-permute-start | bytes 1179656 | tf_op jit(solution)/shard_map/ppermute | solution.py:569
  13.2 14.3 %collective-permute-start.4 = (bf16[128,768]{1,0:T(8,128)(2,1)}, bf16[128,768]{1,0:T(8,128)(2,1)}, u32[]{:S(2)}, u32[]{:S(2)}) collective-permute-start(bf16[128,768]{1,0:T(8,128)(2,1)} %get-tuple-element.90), channel_id=1, source_target_pairs={{0,2},{1,3},{2,0},{3,1},{4,6},{5,7},{6,4},{7,5},{8,10},{9,11},{10,... | collective-permute-start | bytes 589832 | tf_op jit(solution)/shard_map/ppermute | solution.py:569
  13.4 14.2 %collective-permute-start.5 = (bf16[128,768]{1,0:T(8,128)(2,1)}, bf16[128,768]{1,0:T(8,128)(2,1)}, u32[]{:S(2)}, u32[]{:S(2)}) collective-permute-start(bf16[128,768]{1,0:T(8,128)(2,1)} %get-tuple-element.91), channel_id=1, source_target_pairs={{0,6},{1,7},{2,4},{3,5},{4,2},{5,3},{6,0},{7,1},{8,14},{9,15},{10,... | collective-permute-start | bytes 589832 | tf_op jit(solution)/shard_map/ppermute | solution.py:602
  27.0 9.0 %collective-permute-start = (bf16[128,1024]{1,0:T(8,128)(2,1)S(1)}, bf16[128,1024]{1,0:T(8,128)(2,1)S(1)}, u32[]{:S(2)}, u32[]{:S(2)}) collective-permute-start(bf16[128,1024]{1,0:T(8,128)(2,1)S(1)} %bitcast.134), channel_id=1, source_target_pairs={{0,1},{1,0},{2,3},{3,2},{4,5},{5,4},{6,7},{7,6},{8,9},{9,8},{10,11... | collective-permute-start | bytes 786440 | tf_op jit(solution)/shard_map/ppermute | solution.py:569
  27.0 9.0 %collective-permute-start.2 = (bf16[128,1024]{1,0:T(8,128)(2,1)S(1)}, bf16[128,1024]{1,0:T(8,128)(2,1)S(1)}, u32[]{:S(2)}, u32[]{:S(2)}) collective-permute-start(bf16[128,1024]{1,0:T(8,128)(2,1)S(1)} %collective-permute-done.1.refs_2_), channel_id=1, source_target_pairs={{0,1},{1,0},{2,3},{3,2},{4,5},{5,4},{6,7},{7,6},{8,9},{9,8},{10,11... | collective-permute-start | bytes 786440 | tf_op jit(solution)/shard_map/ppermute | solution.py:569
  41.7 24.3 %all-to-all-start = ((bf16[16,80,384]{2,1,0:T(8,128)(2,1)}), bf16[16,80,384]{2,1,0:T(8,128)(2,1)S(1)}, u32[]{:S(2)}, u32[]{:S(2)}) async-start(bf16[16,80,384]{2,1,0:T(8,128)(2,1)} %copy-done.15), calls=%async_computation | async-start | bytes 1966080 | tf_op jit(solution)/shard_map/all_to_all | solution.py:622
  48.8 52.4 %collective-permute-start.17 = (bf16[128,1024]{1,0:T(8,128)(2,1)}, bf16[128,1024]{1,0:T(8,128)(2,1)}, u32[]{:S(2)}, u32[]{:S(2)}) collective-permute-start(bf16[128,1024]{1,0:T(8,128)(2,1)} %bitcast.137), channel_id=1, source_target_pairs={{0,1},{1,0},{2,3},{3,2},{4,5},{5,4},{6,7},{7,6},{8,9},{9,8},{10,11... | collective-permute-start | bytes 786440 | tf_op jit(solution)/shard_map/ppermute | solution.py:569
  48.9 35.9 %collective-permute-start.18 = (bf16[128,1024]{1,0:T(8,128)(2,1)}, bf16[128,1024]{1,0:T(8,128)(2,1)}, u32[]{:S(2)}, u32[]{:S(2)}) collective-permute-start(bf16[128,1024]{1,0:T(8,128)(2,1)} %bitcast.138), channel_id=1, source_target_pairs={{0,2},{1,3},{2,0},{3,1},{4,6},{5,7},{6,4},{7,5},{8,10},{9,11},{10,... | collective-permute-start | bytes 786440 | tf_op jit(solution)/shard_map/ppermute | solution.py:569
  51.5 31.4 %collective-permute-start.13 = (bf16[128,1024]{1,0:T(8,128)(2,1)}, bf16[128,1024]{1,0:T(8,128)(2,1)}, u32[]{:S(2)}, u32[]{:S(2)}) collective-permute-start(bf16[128,1024]{1,0:T(8,128)(2,1)} %get-tuple-element.187), channel_id=1, source_target_pairs={{0,2},{1,3},{2,0},{3,1},{4,6},{5,7},{6,4},{7,5},{8,10},{9,11},{10,... | collective-permute-start | bytes 786440 | tf_op jit(solution)/shard_map/ppermute | solution.py:569
  53.2 31.1 %collective-permute-start.14 = (bf16[128,1024]{1,0:T(8,128)(2,1)}, bf16[128,1024]{1,0:T(8,128)(2,1)}, u32[]{:S(2)}, u32[]{:S(2)}) collective-permute-start(bf16[128,1024]{1,0:T(8,128)(2,1)} %get-tuple-element.186), channel_id=1, source_target_pairs={{0,6},{1,7},{2,4},{3,5},{4,2},{5,3},{6,0},{7,1},{8,14},{9,15},{10,... | collective-permute-start | bytes 786440 | tf_op jit(solution)/shard_map/ppermute | solution.py:602
  66.2 15.7 %collective-permute-start.11 = (bf16[16,80,256]{2,1,0:T(8,128)(2,1)S(1)}, bf16[16,80,256]{2,1,0:T(8,128)(2,1)S(1)}, u32[]{:S(2)}, u32[]{:S(2)}) collective-permute-start(bf16[16,80,256]{2,1,0:T(8,128)(2,1)S(1)} %slice.282), channel_id=1, source_target_pairs={{0,4},{4,0},{8,12},{12,8},{16,20},{20,16},{24,28},{28,24},{32,36},... | collective-permute-start | bytes 1966088 | tf_op jit(solution)/shard_map/ppermute | solution.py:626
  82.0 19.3 %collective-permute-start.12 = (bf16[256,1024]{1,0:T(8,128)(2,1)}, bf16[256,1024]{1,0:T(8,128)(2,1)}, u32[]{:S(2)}, u32[]{:S(2)}) collective-permute-start(bf16[256,1024]{1,0:T(8,128)(2,1)} %get-tuple-element.188), channel_id=1, source_target_pairs={{0,1},{1,0},{2,3},{3,2},{4,5},{5,4},{6,7},{7,6},{8,9},{9,8},{10,11... | collective-permute-start | bytes 1572872 | tf_op jit(solution)/shard_map/ppermute | solution.py:569
  82.9 18.3 %collective-permute-start.15 = (bf16[128,1024]{1,0:T(8,128)(2,1)}, bf16[128,1024]{1,0:T(8,128)(2,1)}, u32[]{:S(2)}, u32[]{:S(2)}) collective-permute-start(bf16[128,1024]{1,0:T(8,128)(2,1)} %get-tuple-element.185), channel_id=1, source_target_pairs={{0,3},{1,2},{2,1},{3,0},{4,7},{5,6},{6,5},{7,4},{8,11},{9,10},{10,... | collective-permute-start | bytes 786440 | tf_op jit(solution)/shard_map/ppermute | solution.py:569
  84.3 16.9 %collective-permute-start.16 = (bf16[128,1024]{1,0:T(8,128)(2,1)}, bf16[128,1024]{1,0:T(8,128)(2,1)}, u32[]{:S(2)}, u32[]{:S(2)}) collective-permute-start(bf16[128,1024]{1,0:T(8,128)(2,1)} %get-tuple-element.184), channel_id=1, source_target_pairs={{0,7},{1,6},{2,5},{3,4},{4,3},{5,2},{6,1},{7,0},{8,15},{9,14},{10,... | collective-permute-start | bytes 786440 | tf_op jit(solution)/shard_map/ppermute | solution.py:603
  84.9 16.4 %collective-permute-start.19 = (bf16[128,1024]{1,0:T(8,128)(2,1)}, bf16[128,1024]{1,0:T(8,128)(2,1)}, u32[]{:S(2)}, u32[]{:S(2)}) collective-permute-start(bf16[128,1024]{1,0:T(8,128)(2,1)} %collective-permute-done.18), channel_id=1, source_target_pairs={{0,1},{1,0},{2,3},{3,2},{4,5},{5,4},{6,7},{7,6},{8,9},{9,8},{10,11... | collective-permute-start | bytes 786440 | tf_op jit(solution)/shard_map/ppermute | solution.py:569
  101.3 13.8 %all-to-all-start.1 = ((bf16[16,64,128]{2,1,0:T(8,128)(2,1)}), bf16[16,64,128]{2,1,0:T(8,128)(2,1)S(1)}, u32[]{:S(2)}, u32[]{:S(2)}) async-start(bf16[16,64,128]{2,1,0:T(8,128)(2,1)} %get-tuple-element.116), calls=%async_computation.1 | async-start | bytes 524288 | tf_op jit(solution)/shard_map/all_to_all | solution.py:622
  118.6 8.6 %collective-permute-start.22 = (bf16[128,1024]{1,0:T(8,128)(2,1)S(1)}, bf16[128,1024]{1,0:T(8,128)(2,1)S(1)}, u32[]{:S(2)}, u32[]{:S(2)}) collective-permute-start(bf16[128,1024]{1,0:T(8,128)(2,1)S(1)} %fusion.24), channel_id=1, source_target_pairs={{0,2},{1,3},{2,0},{3,1},{4,6},{5,7},{6,4},{7,5},{8,10},{9,11},{10,... | collective-permute-start | bytes 786440 | tf_op jit(solution)/shard_map/ppermute | solution.py:569
  147.7 8.8 %collective-permute-start.28 = (bf16[128,1024]{1,0:T(8,128)(2,1)}, bf16[128,1024]{1,0:T(8,128)(2,1)S(1)}, u32[]{:S(2)}, u32[]{:S(2)}) collective-permute-start(bf16[128,1024]{1,0:T(8,128)(2,1)} %fusion.22), channel_id=1, source_target_pairs={{0,2},{1,3},{2,0},{3,1},{4,6},{5,7},{6,4},{7,5},{8,10},{9,11},{10,... | collective-permute-start | bytes 786440 | tf_op jit(solution)/shard_map/ppermute | solution.py:569
  148.6 35.2 %all-to-all-start.2 = ((bf16[16,64,1024]{2,1,0:T(8,128)(2,1)}), bf16[16,64,1024]{2,1,0:T(8,128)(2,1)}, u32[]{:S(2)}, u32[]{:S(2)}) async-start(bf16[16,64,1024]{2,1,0:T(8,128)(2,1)} %bitcast.141), calls=%async_computation.2 | async-start | bytes 4194304 | tf_op jit(solution)/shard_map/all_to_all | solution.py:622
  183.9 15.6 %all-to-all-start.3 = ((bf16[16,64,128]{2,1,0:T(8,128)(2,1)}), bf16[16,64,128]{2,1,0:T(8,128)(2,1)}, u32[]{:S(2)}, u32[]{:S(2)}) async-start(bf16[16,64,128]{2,1,0:T(8,128)(2,1)} %copy-done.12), calls=%async_computation.3 | async-start | bytes 524288 | tf_op jit(solution)/shard_map/all_to_all | solution.py:622
  188.9 132.8 %all-gather.5.cloned.1.call-start = ((), (), s32[]{:S(2)}) async-start(), calls=%async_computation.8 | async-start | bytes 2228224 | tf_op jit(solution)/shard_map/all_gather | solution.py:635
  199.5 44.0 %all-to-all-start.4 = ((bf16[16,80,1024]{2,1,0:T(8,128)(2,1)}), bf16[16,80,1024]{2,1,0:T(8,128)(2,1)}, u32[]{:S(2)}, u32[]{:S(2)}) async-start(bf16[16,80,1024]{2,1,0:T(8,128)(2,1)} %copy-done.1), calls=%async_computation.4 | async-start | bytes 5242880 | tf_op jit(solution)/shard_map/all_to_all | solution.py:622
  220.3 13.5 %collective-permute-start.32 = (bf16[16,64,256]{2,1,0:T(8,128)(2,1)S(1)}, bf16[16,64,256]{2,1,0:T(8,128)(2,1)S(1)}, u32[]{:S(2)}, u32[]{:S(2)}) collective-permute-start(bf16[16,64,256]{2,1,0:T(8,128)(2,1)S(1)} %get-tuple-element.144), channel_id=1, source_target_pairs={{0,4},{4,0},{8,12},{12,8},{16,20},{20,16},{24,28},{28,24},{32,36},... | collective-permute-start | bytes 1572872 | tf_op jit(solution)/shard_map/ppermute | solution.py:626
  248.4 21.4 %all-to-all-start.5 = ((bf16[16,64,384]{2,1,0:T(8,128)(2,1)}), bf16[16,64,384]{2,1,0:T(8,128)(2,1)}, u32[]{:S(2)}, u32[]{:S(2)}) async-start(bf16[16,64,384]{2,1,0:T(8,128)(2,1)} %pad_maximum_fusion.4), calls=%async_computation.5 | async-start | bytes 1572864 | tf_op jit(solution)/shard_map/all_to_all | solution.py:622
  252.7 106.3 %all-gather.7.cloned.1.call-start = ((), (), s32[]{:S(2)}) async-start(), calls=%async_computation.9 | async-start | bytes 2785280 | tf_op jit(solution)/shard_map/all_gather | solution.py:635
  255.3 8.6 %collective-permute-start.51 = (bf16[16,1024]{1,0:T(8,128)(2,1)}, bf16[16,1024]{1,0:T(8,128)(2,1)}, u32[]{:S(2)}, u32[]{:S(2)}) collective-permute-start(bf16[16,1024]{1,0:T(8,128)(2,1)} %get-tuple-element.220), channel_id=1, source_target_pairs={{0,3},{1,2},{2,1},{3,0},{4,7},{5,6},{6,5},{7,4},{8,11},{9,10},{10,... | collective-permute-start | bytes 98312 | tf_op jit(solution)/shard_map/ppermute | solution.py:569
  255.3 8.6 %collective-permute-start.50 = (bf16[16,1024]{1,0:T(8,128)(2,1)S(1)}, bf16[16,1024]{1,0:T(8,128)(2,1)}, u32[]{:S(2)}, u32[]{:S(2)}) collective-permute-start(bf16[16,1024]{1,0:T(8,128)(2,1)S(1)} %get-tuple-element.221), channel_id=1, source_target_pairs={{0,2},{1,3},{2,0},{3,1},{4,6},{5,7},{6,4},{7,5},{8,10},{9,11},{10,... | collective-permute-start | bytes 98312 | tf_op jit(solution)/shard_map/ppermute | solution.py:569
  276.2 8.8 %collective-permute-start.36 = (bf16[128,1024]{1,0:T(8,128)(2,1)S(1)}, bf16[128,1024]{1,0:T(8,128)(2,1)S(1)}, u32[]{:S(2)}, u32[]{:S(2)}) collective-permute-start(bf16[128,1024]{1,0:T(8,128)(2,1)S(1)} %get-tuple-element.208), channel_id=1, source_target_pairs={{0,1},{1,0},{2,3},{3,2},{4,5},{5,4},{6,7},{7,6},{8,9},{9,8},{10,11... | collective-permute-start | bytes 786440 | tf_op jit(solution)/shard_map/ppermute | solution.py:569
  276.8 32.1 %all-to-all-start.6 = ((bf16[16,64,768]{2,1,0:T(8,128)(2,1)}), bf16[16,64,768]{2,1,0:T(8,128)(2,1)}, u32[]{:S(2)}, u32[]{:S(2)}) async-start(bf16[16,64,768]{2,1,0:T(8,128)(2,1)} %copy-done.9), calls=%async_computation.6 | async-start | bytes 3145728 | tf_op jit(solution)/shard_map/all_to_all | solution.py:622
  320.2 9.5 %collective-permute-start.33 = (bf16[128,1024]{1,0:T(8,128)(2,1)}, bf16[128,1024]{1,0:T(8,128)(2,1)}, u32[]{:S(2)}, u32[]{:S(2)}) collective-permute-start(bf16[128,1024]{1,0:T(8,128)(2,1)} %get-tuple-element.210), channel_id=1, source_target_pairs={{0,1},{1,0},{2,3},{3,2},{4,5},{5,4},{6,7},{7,6},{8,9},{9,8},{10,11... | collective-permute-start | bytes 786440 | tf_op jit(solution)/shard_map/ppermute | solution.py:569
  323.1 30.9 %all-to-all-start.7 = ((bf16[16,416,128]{2,1,0:T(8,128)(2,1)}), bf16[16,416,128]{2,1,0:T(8,128)(2,1)}, u32[]{:S(2)}, u32[]{:S(2)}) async-start(bf16[16,416,128]{2,1,0:T(8,128)(2,1)} %broadcast_in_dim.43), calls=%async_computation.7 | async-start | bytes 3407872 | tf_op jit(solution)/shard_map/all_to_all | solution.py:622
  (102 other events, 743.7 us)
Sparse Core Ops, SparseCore 0:
  199.6 69.7 all-gather.4
  271.6 59.0 all-gather.6

commit v2 on v1

--- a/solution.py
+++ b/solution.py
@@ -721,9 +721,10 @@
     hidden = hidden.astype(BF16)
     grad_wdown = dot(hidden, d_down, 0, 0).astype(BF16).reshape(16, 64, 1024)
 
-    (d_pre,) = gelu_back(dot(d_down, w_down, 1, 1))
-    d_pre, grad_wdown = lax.optimization_barrier((d_pre.astype(BF16), grad_wdown))
+    d_output_slots, grad_wdown = lax.optimization_barrier((d_down, grad_wdown))
     grad_wdown = head_exchange(grad_wdown)
+    (d_pre,) = gelu_back(dot(d_output_slots, w_down, 1, 1))
+    d_pre = d_pre.astype(BF16)
     d_normed_two = reduce_slots(dot(d_pre, part_up, 1, 1))
     d_norm_two, grad_gain_two, grad_shift_two = norm_two_back(d_normed_two)
     d_output = cotangent[0].astype(F32)
@@ -751,6 +752,7 @@
     early = plane_sum(early)
     up_rows = to_owners(early[:64], 1).reshape(64, 1024)
     early = plane_gather(jnp.concatenate([up_rows, early[64:].astype(BF16)], axis=0))
+    d_packed, grad_wdown = lax.optimization_barrier((d_packed, grad_wdown))
     d_mixed, late = late_pieces(rank_scalar, d_packed, normed_one)
     late = head_exchange(late)
     d_normed_one = reduce_slots(dot(d_mixed, part_qkv, 1, 1))
@@ -786,12 +788,12 @@
     late, vector = lax.optimization_barrier((late, vector))
     late = to_owners(plane_sum(late), 3).reshape(4, 16, 3, 2, 128)
     late = late.transpose(2, 0, 3, 1, 4).reshape(384, 128)
-    late, grad_wdown = lax.optimization_barrier((late, grad_wdown))
     vector = jnp.pad(vector.astype(BF16), ((0, 8), (0, 0)))
     late = spread(jnp.concatenate([late, vector], axis=0))
 
     out_wdown = grad_wdown.reshape(1024, 1024).astype(F32)
     out_wup, out_wout = spread_early(early)
+    late, out_wup, out_wout = lax.optimization_barrier((late, out_wup, out_wout))
     out_wqkv, out_vec = spread_late(late)
     out_vec = out_vec[:24].reshape(3072)
     return (

time: 378 us -> 372 us (0.984)
  waiting for transfers between devices: 127 us -> 139 us
  local copies, waits for them, and re-layouts: 43.2 us -> 36.3 us
  other arithmetic: 37 us -> 31 us
    all_to_all x8, waiting for transfers between devices: 60.7 us -> 67.9 us  [head_exchange(): lax.all_to_all(value, 'ctx', 0, 0, axis_index_groups=PLANES, tiled=True)]
    unnamed x155 -> x137, local copies, waits for them, and re-layouts: 24.2 us -> 23.6 us
  transfers between devices with their start and end apart: 62 -> 62, of which waited for: 28 -> 33; matrix products, arithmetic and copies ran while one was open for 18% -> 13% of each run, Pallas kernels for 12% -> 11%
where the time goes in v2:
time: 372 us; the launch traced here: 365 us
  waiting for transfers between devices  139 us (37%)
  starting transfers between devices  81.1 us (22%)
  Pallas kernels  46.1 us (12%)
  local copies, waits for them, and re-layouts  36.3 us (10%)
  other arithmetic  31 us (8%)
  between operations  15.7 us (4%)
  matrix products  15.6 us (4%)
    all_to_all x8, waiting for transfers between devices, head_exchange(): lax.all_to_all(value, 'ctx', 0, 0, axis_index_groups=PLANES, tiled=True)  67.9 us
    ppermute x42, waiting for transfers between devices, swap(): return lax.ppermute(value, 'wsh', [(i, i ^ slot) for i in range(4)])  56.1 us
    all_to_all x8, starting transfers between devices, head_exchange(): lax.all_to_all(value, 'ctx', 0, 0, axis_index_groups=PLANES, tiled=True)  41.9 us
    pallas_call x4, Pallas kernels, call_attention(): pl.pallas_call(kernel, out_shape=outs, in_specs=[SMEM] * smem + [VMEM] *...  34.3 us
    unnamed x137, local copies, waits for them, and re-layouts  23.6 us
    ppermute x42, starting transfers between devices, swap(): return lax.ppermute(value, 'wsh', [(i, i ^ slot) for i in range(4)])  19.5 us
    dot_general x8, matrix products, dot(): lax.dot_general(left, right, (((left_dim,), (right_dim,)), ((), ())), pre...  15.6 us
    ppermute x6, starting transfers between devices, partner(): return lax.ppermute(value, 'ctx', [(i, i ^ 1) for i in range(32)])  13.5 us
  transfers between devices with their start and end apart: 62, of which 33 were waited for; matrix products, arithmetic and copies ran while one was open for 13% of the time, Pallas kernels for 11%

profile of v2, /device:TPU:0, one launch (start us, length us, event | category | flops | bytes accessed | tf_op | source)
XLA Modules:
  0.0 364.8 jit_solution(6934662960760930948)
XLA Ops:
  13.4 4.0 %collective-permute-start.5 = (bf16[128,768]{1,0:T(8,128)(2,1)}, bf16[128,768]{1,0:T(8,128)(2,1)}, u32[]{:S(2)}, u32[]{:S(2)}) collective-permute-start(bf16[128,768]{1,0:T(8,128)(2,1)} %get-tuple-element.94), channel_id=1, source_target_pairs={{0,6},{1,7},{2,4},{3,5},{4,2},{5,3},{6,0},{7,1},{8,14},{9,15},{10,... | collective-permute-start | bytes 589832 | tf_op jit(solution)/shard_map/ppermute | solution.py:602
  20.3 3.6 collective-permute-done.9.refs_12_
  28.5 6.1 %collective-permute-done.6.refs_8_ = bf16[128,768]{1,0:T(8,128)(2,1)S(1)} collective-permute-done((bf16[128,768]{1,0:T(8,128)(2,1)}, bf16[128,768]{1,0:T(8,128)(2,1)S(1)}, u32[]{:S(2)}, u32[]{:S(2)}) %collective-permute-start.6) | collective-permute-done | bytes 196640 | tf_op jit(solution)/shard_map/ppermute | solution.py:569
  41.8 7.0 %all-to-all-start = ((bf16[16,80,384]{2,1,0:T(8,128)(2,1)}), bf16[16,80,384]{2,1,0:T(8,128)(2,1)S(1)}, u32[]{:S(2)}, u32[]{:S(2)}) async-start(bf16[16,80,384]{2,1,0:T(8,128)(2,1)} %copy-done.14), calls=%async_computation | async-start | bytes 1966080 | tf_op jit(solution)/shard_map/all_to_all | solution.py:622
  54.9 11.2 %all-to-all-done.own_ref = bf16[16,80,384]{2,1,0:T(8,128)(2,1)S(1)} async-done(((bf16[16,80,384]{2,1,0:T(8,128)(2,1)}), bf16[16,80,384]{2,1,0:T(8,128)(2,1)S(1)}, u32[]{:S(2)}, u32[]{:S(2)}) %all-to-all-start) | async-done | bytes 983072 | tf_op jit(solution)/shard_map/all_to_all | solution.py:622
  67.6 6.4 %shard_map.264 = (s32[80]{0:T(128)S(1)}, bf16[2048,128]{1,0:T(8,128)(2,1)S(1)}, bf16[2048,128]{1,0:T(8,128)(2,1)S(1)}, bf16[2048,64]{1,0:T(8,128)(2,1)S(1)}, f32...) custom-call(s32[1]{0:T(128)} %bitcast.1.head_ref, f32[48]{0:T(128)S(1)} %copy-done.17, ...), custom_call_target="tpu_custom_call" | custom-call | flops 12000000000 | bytes 4000000 | tf_op jit(solution)/shard_map/pallas_call | solution.py:519
  77.2 4.8 %collective-permute-done.11.other_ref = bf16[16,80,256]{2,1,0:T(8,128)(2,1)S(1)} collective-permute-done((bf16[16,80,256]{2,1,0:T(8,128)(2,1)S(1)}, bf16[16,80,256]{2,1,0:T(8,128)(2,1)S(1)}, u32[]{:S(2)}, u32[]{:S(2)}) %collective-permute-start.11) | collective-permute-done | bytes 655392 | tf_op jit(solution)/shard_map/ppermute | solution.py:626
  88.1 10.1 %shard_map.265 = (bf16[16,64,128]{2,1,0:T(8,128)(2,1)}, s32[80]{0:T(128)S(1)}, bf16[2048,128]{1,0:T(8,128)(2,1)S(1)}, bf16[2048,64]{1,0:T(8,128)(2,1)S(1)}, f32[...) custom-call(s32[80]{0:T(128)S(1)} %get-tuple-element.111.own_sorted_ref.sorted_ref, s32[32]{0:T(128)S(1)} %reshape.324.runs_ref, ...), custom_call_target="tpu_custom_call" | custom-call | flops 12000000000 | bytes 4000000 | tf_op jit(solution)/shard_map/pallas_call | solution.py:519
  100.7 5.5 %all-to-all-start.1 = ((bf16[16,64,128]{2,1,0:T(8,128)(2,1)}), bf16[16,64,128]{2,1,0:T(8,128)(2,1)S(1)}, u32[]{:S(2)}, u32[]{:S(2)}) async-start(bf16[16,64,128]{2,1,0:T(8,128)(2,1)} %get-tuple-element.119), calls=%async_computation.1 | async-start | bytes 524288 | tf_op jit(solution)/shard_map/all_to_all | solution.py:622
  106.2 9.0 %all-to-all-done.1.packed_ref = bf16[16,64,128]{2,1,0:T(8,128)(2,1)S(1)} async-done(((bf16[16,64,128]{2,1,0:T(8,128)(2,1)}), bf16[16,64,128]{2,1,0:T(8,128)(2,1)S(1)}, u32[]{:S(2)}, u32[]{:S(2)}) %all-to-all-start.1) | async-done | bytes 262176 | tf_op jit(solution)/shard_map/all_to_all | solution.py:622
  121.8 4.3 %collective-permute-done.22 = bf16[128,1024]{1,0:T(8,128)(2,1)S(1)} collective-permute-done((bf16[128,1024]{1,0:T(8,128)(2,1)S(1)}, bf16[128,1024]{1,0:T(8,128)(2,1)S(1)}, u32[]{:S(2)}, u32[]{:S(2)}) %collective-permute-start.22) | collective-permute-done | bytes 262176 | tf_op jit(solution)/shard_map/ppermute | solution.py:569
  130.1 4.2 %collective-permute-done.24 = bf16[128,1024]{1,0:T(8,128)(2,1)S(1)} collective-permute-done((bf16[128,1024]{1,0:T(8,128)(2,1)S(1)}, bf16[128,1024]{1,0:T(8,128)(2,1)S(1)}, u32[]{:S(2)}, u32[]{:S(2)}) %collective-permute-start.24) | collective-permute-done | bytes 262176 | tf_op jit(solution)/shard_map/ppermute | solution.py:569
  148.7 4.4 %all-to-all-start.2 = ((bf16[16,64,1024]{2,1,0:T(8,128)(2,1)}), bf16[16,64,1024]{2,1,0:T(8,128)(2,1)}, u32[]{:S(2)}, u32[]{:S(2)}) async-start(bf16[16,64,1024]{2,1,0:T(8,128)(2,1)} %bitcast.141), calls=%async_computation.2 | async-start | bytes 4194304 | tf_op jit(solution)/shard_map/all_to_all | solution.py:622
  153.2 3.2 collective-permute-done.28
  159.2 6.6 %collective-permute-done.30 = bf16[128,1024]{1,0:T(8,128)(2,1)S(1)} collective-permute-done((bf16[128,1024]{1,0:T(8,128)(2,1)S(1)}, bf16[128,1024]{1,0:T(8,128)(2,1)S(1)}, u32[]{:S(2)}, u32[]{:S(2)}) %collective-permute-start.30) | collective-permute-done | bytes 262176 | tf_op jit(solution)/shard_map/ppermute | solution.py:569
  168.8 15.5 %all-to-all-done.2 = bf16[16,64,1024]{2,1,0:T(8,128)(2,1)} async-done(((bf16[16,64,1024]{2,1,0:T(8,128)(2,1)}), bf16[16,64,1024]{2,1,0:T(8,128)(2,1)}, u32[]{:S(2)}, u32[]{:S(2)}) %all-to-all-start.2) | async-done | bytes 2097184 | tf_op jit(solution)/shard_map/all_to_all | solution.py:622
  184.4 4.2 %all-to-all-start.3 = ((bf16[16,64,128]{2,1,0:T(8,128)(2,1)}), bf16[16,64,128]{2,1,0:T(8,128)(2,1)}, u32[]{:S(2)}, u32[]{:S(2)}) async-start(bf16[16,64,128]{2,1,0:T(8,128)(2,1)} %copy-done.9), calls=%async_computation.3 | async-start | bytes 524288 | tf_op jit(solution)/shard_map/all_to_all | solution.py:622
  199.4 7.3 %all-to-all-start.4 = ((bf16[16,80,1024]{2,1,0:T(8,128)(2,1)}), bf16[16,80,1024]{2,1,0:T(8,128)(2,1)}, u32[]{:S(2)}, u32[]{:S(2)}) async-start(bf16[16,80,1024]{2,1,0:T(8,128)(2,1)} %copy-done.1), calls=%async_computation.4 | async-start | bytes 5242880 | tf_op jit(solution)/shard_map/all_to_all | solution.py:622
  208.8 10.2 %shard_map.269 = (bf16[16,64,256]{2,1,0:T(8,128)(2,1)S(1)}, f32[64,2048]{1,0:T(8,128)S(1)}, bf16[2048,64]{1,0:T(8,128)(2,1)S(1)}, f32[1,2048]{1,0:T(1,128)S(1)}) custom-call(s32[80]{0:T(128)S(1)} %get-tuple-element.111.own_sorted_ref.sorted_ref, s32[80]{0:T(128)S(1)} %get-tuple-element.121.sorted_ref, bf16[16,64,128]{2,1,0:T(8,128)(2,1)} %all-to-all-done.3.grad_ref, ...), custom_call_target="tpu_custom_call" | custom-call | flops 12000000000 | bytes 4000000 | tf_op jit(solution)/shard_map/pallas_call | solution.py:519
  221.4 7.7 %shard_map.270 = (bf16[16,64,128]{2,1,0:T(8,128)(2,1)S(1)}, f32[16,64,256]{2,1,0:T(8,128)S(1)}) custom-call(s32[80]{0:T(128)S(1)} %get-tuple-element.111.own_sorted_ref.sorted_ref, bf16[2048,64]{1,0:T(8,128)(2,1)S(1)} %get-tuple-element.140.do_ref, bf16[2048,128]{1,0:T(8,128)(2,1)S(1)} %copy-done.20, bf16[2048,128]{1,0:T(8,128)(2,1)S(1)} %copy-done.22, ...), custom_call_target="tpu_custom_call" | custom-call | flops 12000000000 | bytes 4000000 | tf_op jit(solution)/shard_map/pallas_call | solution.py:519
  229.1 3.9 %collective-permute-done.32 = bf16[16,64,256]{2,1,0:T(8,128)(2,1)S(1)} collective-permute-done((bf16[16,64,256]{2,1,0:T(8,128)(2,1)S(1)}, bf16[16,64,256]{2,1,0:T(8,128)(2,1)S(1)}, u32[]{:S(2)}, u32[]{:S(2)}) %collective-permute-start.32) | collective-permute-done | bytes 524320 | tf_op jit(solution)/shard_map/ppermute | solution.py:626
  234.1 8.6 %all-to-all-done.4 = bf16[16,80,1024]{2,1,0:T(8,128)(2,1)} async-done(((bf16[16,80,1024]{2,1,0:T(8,128)(2,1)}), bf16[16,80,1024]{2,1,0:T(8,128)(2,1)}, u32[]{:S(2)}, u32[]{:S(2)}) %all-to-all-start.4) | async-done | bytes 2621472 | tf_op jit(solution)/shard_map/all_to_all | solution.py:622
  246.5 3.9 %all-to-all-start.5 = ((bf16[16,64,384]{2,1,0:T(8,128)(2,1)}), bf16[16,64,384]{2,1,0:T(8,128)(2,1)S(1)}, u32[]{:S(2)}, u32[]{:S(2)}) async-start(bf16[16,64,384]{2,1,0:T(8,128)(2,1)} %pad_maximum_fusion.4), calls=%async_computation.5 | async-start | bytes 1572864 | tf_op jit(solution)/shard_map/all_to_all | solution.py:622
  256.9 11.8 %all-to-all-done.5.packed_ref = bf16[16,64,384]{2,1,0:T(8,128)(2,1)S(1)} async-done(((bf16[16,64,384]{2,1,0:T(8,128)(2,1)}), bf16[16,64,384]{2,1,0:T(8,128)(2,1)S(1)}, u32[]{:S(2)}, u32[]{:S(2)}) %all-to-all-start.5) | async-done | bytes 786464 | tf_op jit(solution)/shard_map/all_to_all | solution.py:622
  275.1 5.0 %all-to-all-start.6 = ((bf16[16,64,768]{2,1,0:T(8,128)(2,1)}), bf16[16,64,768]{2,1,0:T(8,128)(2,1)}, u32[]{:S(2)}, u32[]{:S(2)}) async-start(bf16[16,64,768]{2,1,0:T(8,128)(2,1)} %copy-done.6), calls=%async_computation.6 | async-start | bytes 3145728 | tf_op jit(solution)/shard_map/all_to_all | solution.py:622
  282.8 7.4 %collective-permute-done.39 = bf16[128,1024]{1,0:T(8,128)(2,1)S(1)} collective-permute-done((bf16[128,1024]{1,0:T(8,128)(2,1)}, bf16[128,1024]{1,0:T(8,128)(2,1)S(1)}, u32[]{:S(2)}, u32[]{:S(2)}) %collective-permute-start.39) | collective-permute-done | bytes 262176 | tf_op jit(solution)/shard_map/ppermute | solution.py:569
  302.2 4.8 %all-to-all-done.6 = bf16[16,64,768]{2,1,0:T(8,128)(2,1)} async-done(((bf16[16,64,768]{2,1,0:T(8,128)(2,1)}), bf16[16,64,768]{2,1,0:T(8,128)(2,1)}, u32[]{:S(2)}, u32[]{:S(2)}) %all-to-all-start.6) | async-done | bytes 1572896 | tf_op jit(solution)/shard_map/all_to_all | solution.py:622
  311.4 3.8 %fusion.60 = (bf16[512,1024]{1,0:T(8,128)(2,1)S(1)}, f32[512,1024]{1,0:T(8,128)}) fusion(bf16[512,1024]{1,0:T(8,128)(2,1)} %copy-done.62, bf16[1024,1024]{1,0:T(8,128)(2,1)S(1)} %copy-done), kind=kOutput, calls=%fused_computation.196 | convolution fusion | flops 1074266112 | bytes 6291456 | tf_op jit(solution)/shard_map/dot_general | solution.py:43
  321.1 4.5 %all-to-all-start.7 = ((bf16[16,416,128]{2,1,0:T(8,128)(2,1)}), bf16[16,416,128]{2,1,0:T(8,128)(2,1)}, u32[]{:S(2)}, u32[]{:S(2)}) async-start(bf16[16,416,128]{2,1,0:T(8,128)(2,1)} %broadcast_in_dim.43), calls=%async_computation.7 | async-start | bytes 3407872 | tf_op jit(solution)/shard_map/all_to_all | solution.py:622
  327.8 7.6 %collective-permute-done.35 = bf16[128,1024]{1,0:T(8,128)(2,1)S(1)} collective-permute-done((bf16[128,1024]{1,0:T(8,128)(2,1)S(1)}, bf16[128,1024]{1,0:T(8,128)(2,1)S(1)}, u32[]{:S(2)}, u32[]{:S(2)}) %collective-permute-start.35) | collective-permute-done | bytes 262176 | tf_op jit(solution)/shard_map/ppermute | solution.py:569
  345.4 7.0 %all-to-all-done.7.packed_ref = bf16[16,416,128]{2,1,0:T(8,128)(2,1)} async-done(((bf16[16,416,128]{2,1,0:T(8,128)(2,1)}), bf16[16,416,128]{2,1,0:T(8,128)(2,1)}, u32[]{:S(2)}, u32[]{:S(2)}) %all-to-all-start.7) | async-done | bytes 1703968 | tf_op jit(solution)/shard_map/all_to_all | solution.py:622
  352.5 3.3 shard_map.273
  (346 shorter events, 141.9 us)
Async XLA Ops:
  7.2 19.8 %collective-permute-start.1 = (bf16[128,1024]{1,0:T(8,128)(2,1)}, bf16[128,1024]{1,0:T(8,128)(2,1)S(1)}, u32[]{:S(2)}, u32[]{:S(2)}) collective-permute-start(bf16[128,1024]{1,0:T(8,128)(2,1)} %bitcast.133), channel_id=1, source_target_pairs={{0,2},{1,3},{2,0},{3,1},{4,6},{5,7},{6,4},{7,5},{8,10},{9,11},{10,... | collective-permute-start | bytes 786440 | tf_op jit(solution)/shard_map/ppermute | solution.py:569
  13.2 22.7 %collective-permute-start.3 = (bf16[256,768]{1,0:T(8,128)(2,1)}, bf16[256,768]{1,0:T(8,128)(2,1)S(1)}, u32[]{:S(2)}, u32[]{:S(2)}) collective-permute-start(bf16[256,768]{1,0:T(8,128)(2,1)} %get-tuple-element.92), channel_id=1, source_target_pairs={{0,1},{1,0},{2,3},{3,2},{4,5},{5,4},{6,7},{7,6},{8,9},{9,8},{10,11... | collective-permute-start | bytes 1179656 | tf_op jit(solution)/shard_map/ppermute | solution.py:569
  13.2 14.3 %collective-permute-start.4 = (bf16[128,768]{1,0:T(8,128)(2,1)}, bf16[128,768]{1,0:T(8,128)(2,1)}, u32[]{:S(2)}, u32[]{:S(2)}) collective-permute-start(bf16[128,768]{1,0:T(8,128)(2,1)} %get-tuple-element.93), channel_id=1, source_target_pairs={{0,2},{1,3},{2,0},{3,1},{4,6},{5,7},{6,4},{7,5},{8,10},{9,11},{10,... | collective-permute-start | bytes 589832 | tf_op jit(solution)/shard_map/ppermute | solution.py:569
  13.4 14.2 %collective-permute-start.5 = (bf16[128,768]{1,0:T(8,128)(2,1)}, bf16[128,768]{1,0:T(8,128)(2,1)}, u32[]{:S(2)}, u32[]{:S(2)}) collective-permute-start(bf16[128,768]{1,0:T(8,128)(2,1)} %get-tuple-element.94), channel_id=1, source_target_pairs={{0,6},{1,7},{2,4},{3,5},{4,2},{5,3},{6,0},{7,1},{8,14},{9,15},{10,... | collective-permute-start | bytes 589832 | tf_op jit(solution)/shard_map/ppermute | solution.py:602
  27.0 9.0 %collective-permute-start = (bf16[128,1024]{1,0:T(8,128)(2,1)S(1)}, bf16[128,1024]{1,0:T(8,128)(2,1)S(1)}, u32[]{:S(2)}, u32[]{:S(2)}) collective-permute-start(bf16[128,1024]{1,0:T(8,128)(2,1)S(1)} %bitcast.134), channel_id=1, source_target_pairs={{0,1},{1,0},{2,3},{3,2},{4,5},{5,4},{6,7},{7,6},{8,9},{9,8},{10,11... | collective-permute-start | bytes 786440 | tf_op jit(solution)/shard_map/ppermute | solution.py:569
  27.0 9.0 %collective-permute-start.2 = (bf16[128,1024]{1,0:T(8,128)(2,1)S(1)}, bf16[128,1024]{1,0:T(8,128)(2,1)S(1)}, u32[]{:S(2)}, u32[]{:S(2)}) collective-permute-start(bf16[128,1024]{1,0:T(8,128)(2,1)S(1)} %collective-permute-done.1.refs_2_), channel_id=1, source_target_pairs={{0,1},{1,0},{2,3},{3,2},{4,5},{5,4},{6,7},{7,6},{8,9},{9,8},{10,11... | collective-permute-start | bytes 786440 | tf_op jit(solution)/shard_map/ppermute | solution.py:569
  27.6 8.4 %collective-permute-start.7 = (bf16[128,768]{1,0:T(8,128)(2,1)}, bf16[128,768]{1,0:T(8,128)(2,1)S(1)}, u32[]{:S(2)}, u32[]{:S(2)}) collective-permute-start(bf16[128,768]{1,0:T(8,128)(2,1)} %get-tuple-element.96), channel_id=1, source_target_pairs={{0,7},{1,6},{2,5},{3,4},{4,3},{5,2},{6,1},{7,0},{8,15},{9,14},{10,... | collective-permute-start | bytes 589832 | tf_op jit(solution)/shard_map/ppermute | solution.py:603
  41.8 24.3 %all-to-all-start = ((bf16[16,80,384]{2,1,0:T(8,128)(2,1)}), bf16[16,80,384]{2,1,0:T(8,128)(2,1)S(1)}, u32[]{:S(2)}, u32[]{:S(2)}) async-start(bf16[16,80,384]{2,1,0:T(8,128)(2,1)} %copy-done.14), calls=%async_computation | async-start | bytes 1966080 | tf_op jit(solution)/shard_map/all_to_all | solution.py:622
  48.9 51.8 %collective-permute-start.17 = (bf16[128,1024]{1,0:T(8,128)(2,1)}, bf16[128,1024]{1,0:T(8,128)(2,1)}, u32[]{:S(2)}, u32[]{:S(2)}) collective-permute-start(bf16[128,1024]{1,0:T(8,128)(2,1)} %bitcast.137), channel_id=1, source_target_pairs={{0,1},{1,0},{2,3},{3,2},{4,5},{5,4},{6,7},{7,6},{8,9},{9,8},{10,11... | collective-permute-start | bytes 786440 | tf_op jit(solution)/shard_map/ppermute | solution.py:569
  49.0 35.9 %collective-permute-start.18 = (bf16[128,1024]{1,0:T(8,128)(2,1)}, bf16[128,1024]{1,0:T(8,128)(2,1)}, u32[]{:S(2)}, u32[]{:S(2)}) collective-permute-start(bf16[128,1024]{1,0:T(8,128)(2,1)} %bitcast.138), channel_id=1, source_target_pairs={{0,2},{1,3},{2,0},{3,1},{4,6},{5,7},{6,4},{7,5},{8,10},{9,11},{10,... | collective-permute-start | bytes 786440 | tf_op jit(solution)/shard_map/ppermute | solution.py:569
  51.6 31.4 %collective-permute-start.13 = (bf16[128,1024]{1,0:T(8,128)(2,1)}, bf16[128,1024]{1,0:T(8,128)(2,1)}, u32[]{:S(2)}, u32[]{:S(2)}) collective-permute-start(bf16[128,1024]{1,0:T(8,128)(2,1)} %get-tuple-element.193), channel_id=1, source_target_pairs={{0,2},{1,3},{2,0},{3,1},{4,6},{5,7},{6,4},{7,5},{8,10},{9,11},{10,... | collective-permute-start | bytes 786440 | tf_op jit(solution)/shard_map/ppermute | solution.py:569
  53.3 31.1 %collective-permute-start.14 = (bf16[128,1024]{1,0:T(8,128)(2,1)}, bf16[128,1024]{1,0:T(8,128)(2,1)}, u32[]{:S(2)}, u32[]{:S(2)}) collective-permute-start(bf16[128,1024]{1,0:T(8,128)(2,1)} %get-tuple-element.192), channel_id=1, source_target_pairs={{0,6},{1,7},{2,4},{3,5},{4,2},{5,3},{6,0},{7,1},{8,14},{9,15},{10,... | collective-permute-start | bytes 786440 | tf_op jit(solution)/shard_map/ppermute | solution.py:602
  66.3 15.7 %collective-permute-start.11 = (bf16[16,80,256]{2,1,0:T(8,128)(2,1)S(1)}, bf16[16,80,256]{2,1,0:T(8,128)(2,1)S(1)}, u32[]{:S(2)}, u32[]{:S(2)}) collective-permute-start(bf16[16,80,256]{2,1,0:T(8,128)(2,1)S(1)} %slice.282), channel_id=1, source_target_pairs={{0,4},{4,0},{8,12},{12,8},{16,20},{20,16},{24,28},{28,24},{32,36},... | collective-permute-start | bytes 1966088 | tf_op jit(solution)/shard_map/ppermute | solution.py:626
  82.0 18.6 %collective-permute-start.12 = (bf16[256,1024]{1,0:T(8,128)(2,1)}, bf16[256,1024]{1,0:T(8,128)(2,1)}, u32[]{:S(2)}, u32[]{:S(2)}) collective-permute-start(bf16[256,1024]{1,0:T(8,128)(2,1)} %get-tuple-element.194), channel_id=1, source_target_pairs={{0,1},{1,0},{2,3},{3,2},{4,5},{5,4},{6,7},{7,6},{8,9},{9,8},{10,11... | collective-permute-start | bytes 1572872 | tf_op jit(solution)/shard_map/ppermute | solution.py:569
  83.0 17.6 %collective-permute-start.15 = (bf16[128,1024]{1,0:T(8,128)(2,1)}, bf16[128,1024]{1,0:T(8,128)(2,1)}, u32[]{:S(2)}, u32[]{:S(2)}) collective-permute-start(bf16[128,1024]{1,0:T(8,128)(2,1)} %get-tuple-element.191), channel_id=1, source_target_pairs={{0,3},{1,2},{2,1},{3,0},{4,7},{5,6},{6,5},{7,4},{8,11},{9,10},{10,... | collective-permute-start | bytes 786440 | tf_op jit(solution)/shard_map/ppermute | solution.py:569
  84.4 16.3 %collective-permute-start.16 = (bf16[128,1024]{1,0:T(8,128)(2,1)}, bf16[128,1024]{1,0:T(8,128)(2,1)}, u32[]{:S(2)}, u32[]{:S(2)}) collective-permute-start(bf16[128,1024]{1,0:T(8,128)(2,1)} %get-tuple-element.190), channel_id=1, source_target_pairs={{0,7},{1,6},{2,5},{3,4},{4,3},{5,2},{6,1},{7,0},{8,15},{9,14},{10,... | collective-permute-start | bytes 786440 | tf_op jit(solution)/shard_map/ppermute | solution.py:603
  84.9 15.7 %collective-permute-start.19 = (bf16[128,1024]{1,0:T(8,128)(2,1)}, bf16[128,1024]{1,0:T(8,128)(2,1)}, u32[]{:S(2)}, u32[]{:S(2)}) collective-permute-start(bf16[128,1024]{1,0:T(8,128)(2,1)} %collective-permute-done.18), channel_id=1, source_target_pairs={{0,1},{1,0},{2,3},{3,2},{4,5},{5,4},{6,7},{7,6},{8,9},{9,8},{10,11... | collective-permute-start | bytes 786440 | tf_op jit(solution)/shard_map/ppermute | solution.py:569
  100.7 14.5 %all-to-all-start.1 = ((bf16[16,64,128]{2,1,0:T(8,128)(2,1)}), bf16[16,64,128]{2,1,0:T(8,128)(2,1)S(1)}, u32[]{:S(2)}, u32[]{:S(2)}) async-start(bf16[16,64,128]{2,1,0:T(8,128)(2,1)} %get-tuple-element.119), calls=%async_computation.1 | async-start | bytes 524288 | tf_op jit(solution)/shard_map/all_to_all | solution.py:622
  117.7 8.4 %collective-permute-start.22 = (bf16[128,1024]{1,0:T(8,128)(2,1)S(1)}, bf16[128,1024]{1,0:T(8,128)(2,1)S(1)}, u32[]{:S(2)}, u32[]{:S(2)}) collective-permute-start(bf16[128,1024]{1,0:T(8,128)(2,1)S(1)} %fusion.24), channel_id=1, source_target_pairs={{0,2},{1,3},{2,0},{3,1},{4,6},{5,7},{6,4},{7,5},{8,10},{9,11},{10,... | collective-permute-start | bytes 786440 | tf_op jit(solution)/shard_map/ppermute | solution.py:569
  147.8 8.6 %collective-permute-start.28 = (bf16[128,1024]{1,0:T(8,128)(2,1)}, bf16[128,1024]{1,0:T(8,128)(2,1)S(1)}, u32[]{:S(2)}, u32[]{:S(2)}) collective-permute-start(bf16[128,1024]{1,0:T(8,128)(2,1)} %fusion.22), channel_id=1, source_target_pairs={{0,2},{1,3},{2,0},{3,1},{4,6},{5,7},{6,4},{7,5},{8,10},{9,11},{10,... | collective-permute-start | bytes 786440 | tf_op jit(solution)/shard_map/ppermute | solution.py:569
  148.7 35.7 %all-to-all-start.2 = ((bf16[16,64,1024]{2,1,0:T(8,128)(2,1)}), bf16[16,64,1024]{2,1,0:T(8,128)(2,1)}, u32[]{:S(2)}, u32[]{:S(2)}) async-start(bf16[16,64,1024]{2,1,0:T(8,128)(2,1)} %bitcast.141), calls=%async_computation.2 | async-start | bytes 4194304 | tf_op jit(solution)/shard_map/all_to_all | solution.py:622
  184.4 15.0 %all-to-all-start.3 = ((bf16[16,64,128]{2,1,0:T(8,128)(2,1)}), bf16[16,64,128]{2,1,0:T(8,128)(2,1)}, u32[]{:S(2)}, u32[]{:S(2)}) async-start(bf16[16,64,128]{2,1,0:T(8,128)(2,1)} %copy-done.9), calls=%async_computation.3 | async-start | bytes 524288 | tf_op jit(solution)/shard_map/all_to_all | solution.py:622
  188.6 80.7 %all-gather.5.cloned.1.call-start = ((), (), s32[]{:S(2)}) async-start(), calls=%async_computation.8 | async-start | bytes 2228224 | tf_op jit(solution)/shard_map/all_gather | solution.py:635
  199.4 43.3 %all-to-all-start.4 = ((bf16[16,80,1024]{2,1,0:T(8,128)(2,1)}), bf16[16,80,1024]{2,1,0:T(8,128)(2,1)}, u32[]{:S(2)}, u32[]{:S(2)}) async-start(bf16[16,80,1024]{2,1,0:T(8,128)(2,1)} %copy-done.1), calls=%async_computation.4 | async-start | bytes 5242880 | tf_op jit(solution)/shard_map/all_to_all | solution.py:622
  219.0 14.0 %collective-permute-start.32 = (bf16[16,64,256]{2,1,0:T(8,128)(2,1)S(1)}, bf16[16,64,256]{2,1,0:T(8,128)(2,1)S(1)}, u32[]{:S(2)}, u32[]{:S(2)}) collective-permute-start(bf16[16,64,256]{2,1,0:T(8,128)(2,1)S(1)} %get-tuple-element.147), channel_id=1, source_target_pairs={{0,4},{4,0},{8,12},{12,8},{16,20},{20,16},{24,28},{28,24},{32,36},... | collective-permute-start | bytes 1572872 | tf_op jit(solution)/shard_map/ppermute | solution.py:626
  246.5 22.3 %all-to-all-start.5 = ((bf16[16,64,384]{2,1,0:T(8,128)(2,1)}), bf16[16,64,384]{2,1,0:T(8,128)(2,1)S(1)}, u32[]{:S(2)}, u32[]{:S(2)}) async-start(bf16[16,64,384]{2,1,0:T(8,128)(2,1)} %pad_maximum_fusion.4), calls=%async_computation.5 | async-start | bytes 1572864 | tf_op jit(solution)/shard_map/all_to_all | solution.py:622
  250.4 90.6 %all-gather.7.cloned.1.call-start = ((), (), s32[]{:S(2)}) async-start(), calls=%async_computation.9 | async-start | bytes 2785280 | tf_op jit(solution)/shard_map/all_gather | solution.py:635
  274.5 8.3 %collective-permute-start.37 = (bf16[128,1024]{1,0:T(8,128)(2,1)S(1)}, bf16[128,1024]{1,0:T(8,128)(2,1)S(1)}, u32[]{:S(2)}, u32[]{:S(2)}) collective-permute-start(bf16[128,1024]{1,0:T(8,128)(2,1)S(1)} %get-tuple-element.214), channel_id=1, source_target_pairs={{0,1},{1,0},{2,3},{3,2},{4,5},{5,4},{6,7},{7,6},{8,9},{9,8},{10,11... | collective-permute-start | bytes 786440 | tf_op jit(solution)/shard_map/ppermute | solution.py:569
  275.1 31.9 %all-to-all-start.6 = ((bf16[16,64,768]{2,1,0:T(8,128)(2,1)}), bf16[16,64,768]{2,1,0:T(8,128)(2,1)}, u32[]{:S(2)}, u32[]{:S(2)}) async-start(bf16[16,64,768]{2,1,0:T(8,128)(2,1)} %copy-done.6), calls=%async_computation.6 | async-start | bytes 3145728 | tf_op jit(solution)/shard_map/all_to_all | solution.py:622
  318.1 9.8 %collective-permute-start.33 = (bf16[128,1024]{1,0:T(8,128)(2,1)}, bf16[128,1024]{1,0:T(8,128)(2,1)}, u32[]{:S(2)}, u32[]{:S(2)}) collective-permute-start(bf16[128,1024]{1,0:T(8,128)(2,1)} %get-tuple-element.216), channel_id=1, source_target_pairs={{0,1},{1,0},{2,3},{3,2},{4,5},{5,4},{6,7},{7,6},{8,9},{9,8},{10,11... | collective-permute-start | bytes 786440 | tf_op jit(solution)/shard_map/ppermute | solution.py:569
  321.1 31.4 %all-to-all-start.7 = ((bf16[16,416,128]{2,1,0:T(8,128)(2,1)}), bf16[16,416,128]{2,1,0:T(8,128)(2,1)}, u32[]{:S(2)}, u32[]{:S(2)}) async-start(bf16[16,416,128]{2,1,0:T(8,128)(2,1)} %broadcast_in_dim.43), calls=%async_computation.7 | async-start | bytes 3407872 | tf_op jit(solution)/shard_map/all_to_all | solution.py:622
  327.0 8.4 %collective-permute-start.35 = (bf16[128,1024]{1,0:T(8,128)(2,1)S(1)}, bf16[128,1024]{1,0:T(8,128)(2,1)S(1)}, u32[]{:S(2)}, u32[]{:S(2)}) collective-permute-start(bf16[128,1024]{1,0:T(8,128)(2,1)S(1)} %fusion.17), channel_id=1, source_target_pairs={{0,2},{1,3},{2,0},{3,1},{4,6},{5,7},{6,4},{7,5},{8,10},{9,11},{10,... | collective-permute-start | bytes 786440 | tf_op jit(solution)/shard_map/ppermute | solution.py:569
  (93 other events, 606.1 us)
Sparse Core Ops, SparseCore 0:
  199.5 69.7 all-gather.4
  271.5 62.1 all-gather.6
